TPU v7x, 32 devices: a whole 2x2x4 slice. The times are simulated.
32 devices in a mesh: rep: 2 (over x), attn: 2 (over core), ffn: 8 (over z, y).
Axes of the slice: x: 2, y: 2, z: 4, core: 2. Of those that a mesh axis runs over, the one named last changes fastest.
Arguments:
- queries: bfloat16 [256, 2, 4096], P(('rep', 'attn', 'ffn')), parts along dimension 0, may hold values from -8 to 8
- new_keys: bfloat16 [256, 2, 512], P(('rep', 'attn', 'ffn')), parts along dimension 0, may hold values from -6 to 6
- new_values: bfloat16 [256, 2, 512], P(('rep', 'attn', 'ffn')), parts along dimension 0, may hold values from -6 to 6
- key_cache: bfloat16 [256, 256, 512], P(('rep', 'attn', 'ffn')), parts along dimension 0, may hold values from -6 to 6
- value_cache: bfloat16 [256, 256, 512], P(('rep', 'attn', 'ffn')), parts along dimension 0, may hold values from -6 to 6
- residual_in: bfloat16 [256, 2, 4096], P(('rep', 'attn', 'ffn')), parts along dimension 0, may hold values from -40 to 40
- norm_gain: bfloat16 [4096], replicated, may hold values from 0.099609375 to 1.8984375
- gate_weight: bfloat16 [4096, 14336], P(None, ('attn', 'ffn')), may hold values from -0.09375 to 0.09375
- up_weight: bfloat16 [4096, 14336], P(None, ('attn', 'ffn')), may hold values from -0.09375 to 0.09375
- down_weight: bfloat16 [14336, 4096], P(('attn', 'ffn')), may hold values from -0.046875 to 0.046875
- live_counts: int32 [32], P(('rep', 'attn', 'ffn')), parts along dimension 0, may hold values from 6 to 8, as said below
- cache_lengths: int32 [256], P(('rep', 'attn', 'ffn')), parts along dimension 0, may hold values from 2 to 256, as said below
- positions: int32 [256], P(('rep', 'attn', 'ffn')), parts along dimension 0, may hold values from 256 to 1023
Outputs:
- layer_out: bfloat16 [256, 2, 4096], P(('rep', 'attn', 'ffn')), parts along dimension 0
There are 2 independent parts, one for each index of `rep`. A program takes and returns all parts, laid end to end along the dimension named above; an argument that names none is the same for every part. Nothing has to cross between parts.
Inputs may be any that keep to these rules, and one draw needn't show every extreme that they name: `live_counts`: some attention rank holds exactly 8 live requests. `cache_lengths`: some request has exactly 256 cached keys.
All inputs are finite; a program needn't handle non-finite values.
Results may differ from a plain program's by a relative error of at most 0.0065.
Values may be sent and summed in bfloat16 or wider, within the bound.
A program may use at most 128 MiB of HBM per device.

v0:
```python
import jax
import jax.numpy as jnp
from jax import lax
from jax.sharding import PartitionSpec as P

HEADS = 32
KVH = 4
HD = 128


rope_base = 500000.0
norm_epsilon = 1e-05


def rotate_heads(values, angles):
    middle = values.shape[-1] // 2
    cosine = jnp.cos(angles)
    sine = jnp.sin(angles)
    first = values[..., :middle]
    second = values[..., middle:]
    return jnp.concatenate(
        [first * cosine - second * sine, second * cosine + first * sine], axis=-1
    )


def attend(queries, new_keys, new_values, key_cache, value_cache, cache_lengths, positions):
    requests = queries.shape[0]
    drafts = queries.shape[1]
    cache_slots = key_cache.shape[1]
    group_size = HEADS // KVH
    frequency = rope_base ** (-2.0 * jnp.arange(HD // 2, dtype=jnp.float32) / HD)
    offsets = (
        positions.astype(jnp.float32)[:, None] + jnp.arange(drafts, dtype=jnp.float32)[None, :]
    )
    angles = offsets[:, :, None, None] * frequency
    rotated_queries = rotate_heads(
        queries.astype(jnp.float32).reshape(requests, drafts, HEADS, HD), angles
    )
    rotated_queries = rotated_queries.astype(jnp.bfloat16).reshape(
        requests, drafts, KVH, group_size, HD
    )
    rotated_keys = rotate_heads(
        new_keys.astype(jnp.float32).reshape(requests, drafts, KVH, HD), angles
    )
    rotated_keys = rotated_keys.astype(jnp.bfloat16)
    cached_keys = key_cache.reshape(requests, cache_slots, KVH, HD)
    cached_values = value_cache.reshape(requests, cache_slots, KVH, HD)
    fresh_values = new_values.reshape(requests, drafts, KVH, HD)
    score_scale = HD ** (-0.5)
    cache_scores = (
        jnp.einsum(
            "rsgqd,rlgd->rgsql", rotated_queries, cached_keys, preferred_element_type=jnp.float32
        )
        * score_scale
    )
    draft_scores = (
        jnp.einsum(
            "rsgqd,rtgd->rgsqt", rotated_queries, rotated_keys, preferred_element_type=jnp.float32
        )
        * score_scale
    )
    cache_mask = (jnp.arange(cache_slots)[None, :] < cache_lengths[:, None])[:, None, None, None, :]
    draft_mask = (jnp.arange(drafts)[None, :] <= jnp.arange(drafts)[:, None])[
        None, None, :, None, :
    ]
    cache_scores = jnp.where(cache_mask, cache_scores, -jnp.inf)
    draft_scores = jnp.where(draft_mask, draft_scores, -jnp.inf)
    highest = jnp.maximum(jnp.max(cache_scores, axis=-1), jnp.max(draft_scores, axis=-1))[..., None]
    cache_exp = jnp.exp(cache_scores - highest)
    draft_exp = jnp.exp(draft_scores - highest)
    denominator = jnp.sum(cache_exp, axis=-1, keepdims=True) + jnp.sum(
        draft_exp, axis=-1, keepdims=True
    )
    cache_weights = (cache_exp / denominator).astype(jnp.bfloat16)
    draft_weights = (draft_exp / denominator).astype(jnp.bfloat16)
    mixed = jnp.einsum(
        "rgsql,rlgd->rsgqd", cache_weights, cached_values, preferred_element_type=jnp.float32
    )
    mixed = mixed + jnp.einsum(
        "rgsqt,rtgd->rsgqd", draft_weights, fresh_values, preferred_element_type=jnp.float32
    )
    return mixed.reshape(requests, drafts, HEADS * HD)


def normalize(stream, norm_gain):
    values = stream.astype(jnp.float32)
    mean_square = jnp.mean(values * values, axis=-1, keepdims=True)
    return (values * lax.rsqrt(mean_square + norm_epsilon) * norm_gain.astype(jnp.float32)).astype(
        jnp.bfloat16
    )


def feed_forward_rows(picked, gate_weight, up_weight, down_weight):
    gate_proj = jnp.dot(picked, gate_weight, preferred_element_type=jnp.float32)
    up_proj = jnp.dot(picked, up_weight, preferred_element_type=jnp.float32)
    hidden = (jax.nn.silu(gate_proj) * up_proj).astype(jnp.bfloat16)
    return jnp.dot(hidden, down_weight, preferred_element_type=jnp.float32)


def term_maker(gathered, gate_weight, up_weight, down_weight):

    def compute(row_start, row_count):
        return feed_forward_rows(gathered, gate_weight, up_weight, down_weight)

    return compute


def shards(
    queries,
    new_keys,
    new_values,
    key_cache,
    value_cache,
    residual_in,
    norm_gain,
    gate_weight,
    up_weight,
    down_weight,
    live_counts,
    cache_lengths,
    positions,
):
    requests = residual_in.shape[0]
    drafts = residual_in.shape[1]
    model_width = residual_in.shape[2]
    attention = attend(
        queries, new_keys, new_values, key_cache, value_cache, cache_lengths, positions
    )
    stream = lax.optimization_barrier(
        (residual_in.astype(jnp.float32) + attention).astype(jnp.bfloat16)
    )
    normed = normalize(stream, norm_gain).reshape(requests * drafts, model_width)
    gathered = lax.all_gather(normed, ("attn", "ffn"), axis=0, tiled=True)
    compute = term_maker(gathered, gate_weight, up_weight, down_weight)
    feed = lax.psum_scatter(
        compute(jnp.int32(0), requests * drafts * lax.axis_size(("attn", "ffn"))),
        ("attn", "ffn"),
        scatter_dimension=0,
        tiled=True,
    )
    live_slot = jnp.arange(requests) < live_counts[0]
    combined = (stream.astype(jnp.float32) + feed.reshape(requests, drafts, model_width)).astype(
        jnp.bfloat16
    )
    return jnp.where(live_slot[:, None, None], combined, jnp.zeros_like(combined))


def solution(mesh):
    return jax.shard_map(
        shards,
        mesh=mesh,
        in_specs=(
            P(("rep", "attn", "ffn"), None, None),
            P(("rep", "attn", "ffn"), None, None),
            P(("rep", "attn", "ffn"), None, None),
            P(("rep", "attn", "ffn"), None, None),
            P(("rep", "attn", "ffn"), None, None),
            P(("rep", "attn", "ffn"), None, None),
            P(),
            P(None, ("attn", "ffn")),
            P(None, ("attn", "ffn")),
            P(("attn", "ffn"), None),
            P(("rep", "attn", "ffn")),
            P(("rep", "attn", "ffn")),
            P(("rep", "attn", "ffn")),
        ),
        out_specs=P(("rep", "attn", "ffn"), None, None),
        check_vma=False,
    )
```

profile of v0, /device:TPU:0, one launch (start us, length us, event | category | flops | bytes accessed | tf_op | source)
XLA Modules:
  0.0 161.5 jit_solution(6265684789671068513)
XLA Ops:
  6.5 0.0 copy-start
  6.5 0.0 all-gather.2.cloned.1.call-start
  6.6 0.7 convert_element_type.37
  7.2 0.1 iota_add_fusion
  7.3 1.0 reshape.135
  8.3 0.7 bitcast_convert_fusion
  9.0 0.2 multiply_cosine_fusion
  9.2 0.2 fusion.27
  9.4 0.1 subtract_convert_fusion.1
  9.5 0.0 copy-start.3
  9.5 2.6 %reshape.126 = bf16[8,256,4,128]{3,2,1,0:T(4,128)(2,1)S(1)} reshape(bf16[8,256,512]{2,1,0:T(8,128)(2,1)} %param.16) | data formatting | bytes 4194304 | tf_op jit(solution)/shard_map/reshape | solution.py:46
  12.1 0.0 copy-done.3
  12.1 0.1 iota_compare_fusion
  12.2 0.8 fusion.41
  12.9 0.8 fusion.42
  13.8 0.1 fusion.32
  13.9 0.3 fusion.19
  14.2 2.6 %reshape.129 = bf16[8,256,4,128]{3,2,1,0:T(4,128)(2,1)S(1)} reshape(bf16[8,256,512]{2,1,0:T(8,128)(2,1)} %param.17) | data formatting | bytes 4194304 | tf_op jit(solution)/shard_map/reshape | solution.py:47
  16.8 0.0 copy-done
  16.8 0.3 fusion.33
  17.1 0.0 copy-start.1
  17.1 0.0 copy-start.2
  17.1 0.5 fusion.14
  17.6 0.1 reshape.131
  17.6 0.3 copy-done.1
  18.0 0.1 add_convert_fusion
  18.1 0.1 fusion.21
  18.2 0.0 copy-done.2
  18.2 0.1 fusion.23
  18.3 0.1 copy.33
  18.5 0.7 reshape.132
  19.2 0.0 all-gather.2.cloned.1.call-update
  19.2 0.0 reduce-scatter.2.cloned.1.call-start
  19.2 44.2 %all-gather.2.cloned.1.call-done = bf16[256,4096]{1,0:T(8,128)(2,1)} async-done(((bf16[16,4096]{1,0:T(8,128)(2,1)}), bf16[256,4096]{1,0:T(8,128)(2,1)}) %all-gather.2.cloned.1.call-update) | async-done | bytes 2097168 | tf_op jit(solution)/shard_map/all_gather | solution.py:133
  63.4 0.0 copy-start.4
  63.4 6.2 %fusion.43 = f32[256,896]{1,0:T(8,128)S(1)} fusion(bf16[256,4096]{1,0:T(8,128)(2,1)} %all-gather.2.cloned.1.call-done, bf16[4096,896]{1,0:T(8,128)(2,1)} %param.20), kind=kOutput, calls=%fused_computation.60 | convolution fusion | flops 1879048192 | bytes 10354688 | tf_op jit(solution)/shard_map/dot_general | solution.py:94
  69.6 0.0 copy-done.4
  69.7 11.7 %fusion.18 = f32[256,4096]{1,0:T(8,128)} fusion(bf16[896,4096]{1,0:T(8,128)(2,1)} %param.22, bf16[256,4096]{1,0:T(8,128)(2,1)S(1)} %copy-done.4, bf16[4096,896]{1,0:T(8,128)(2,1)} %param.21, f32[256,896]{1,0:T(8,128)S(1)} %fusion.43), kind=kOutput, calls=%fused_computation.12 | convolution fusion | flops 3759472640 | bytes 21889024 | tf_op jit(solution)/shard_map/dot_general | solution.py:97
  81.3 0.0 reduce-scatter.2.cloned.1.call-update
  82.0 70.6 %reduce-scatter.2.cloned.1.call-done = f32[16,4096]{1,0:T(8,128)} async-done(((f32[256,4096]{1,0:T(8,128)}), f32[16,4096]{1,0:T(8,128)}) %reduce-scatter.2.cloned.1.call-update) | async-done | bytes 262160 | tf_op jit(solution)/shard_map/reduce_scatter | solution.py:135
  152.6 1.1 reshape.133
  153.7 0.2 fusion.29
  153.9 0.8 copy.35
  (8 shorter events, 0.1 us)
Async XLA Ops:
  6.5 10.3 %copy-start = (bf16[8,2,512]{2,1,0:T(2,128)(2,1)S(1)}, bf16[8,2,512]{2,1,0:T(2,128)(2,1)}, u32[]{:S(2)}) copy-start(bf16[8,2,512]{2,1,0:T(2,128)(2,1)} %param.15) | copy-start | bytes 49156
  6.5 56.9 %all-gather.2.cloned.1.call-start = ((), (), s32[]{:S(2)}) async-start(), calls=%async_computation.1 | async-start | bytes 2228224 | tf_op jit(solution)/shard_map/all_gather | solution.py:133
  9.5 2.6 %copy-start.3 = (s32[8]{0:T(128)S(1)}, s32[8]{0:T(128)}, u32[]{:S(2)}) copy-start(s32[8]{0:T(128)} %param.24) | copy-start | bytes 100
  17.1 0.9 copy-start.1
  17.1 1.1 copy-start.2
  19.2 133.4 %reduce-scatter.2.cloned.1.call-start = ((), (), s32[]{:S(2)}) async-start(), calls=%async_computation.2 | async-start | bytes 4456448 | tf_op jit(solution)/shard_map/reduce_scatter | solution.py:135
  63.4 6.2 %copy-start.4 = (bf16[256,4096]{1,0:T(8,128)(2,1)S(1)}, bf16[256,4096]{1,0:T(8,128)(2,1)}, u32[]{:S(2)}) copy-start(bf16[256,4096]{1,0:T(8,128)(2,1)} %all-gather.2.cloned.1.call-done) | copy-start | bytes 6291460
Sparse Core Ops, SparseCore 0:
  19.3 44.0 all-gather.1
  81.5 71.0 reduce-scatter.1
where the time goes:
time: 162 us
  waiting for transfers between devices  115 us (71%)
  matrix products  20.1 us (12%)
  between operations  14.2 us (9%)
  local copies, waits for them, and re-layouts  9.28 us (6%)
  other arithmetic  2.98 us (2%)
    reduce_scatter x1, waiting for transfers between devices, shards(): lax.psum_scatter(compute(jnp.int32(0), requests * drafts * lax.axis_size(...  70.6 us
    all_gather x1, waiting for transfers between devices, shards(): gathered = lax.all_gather(normed, ('attn', 'ffn'), axis=0, tiled=True)  44.2 us
    dot_general x1, matrix products, feed_forward_rows(): return jnp.dot(hidden, down_weight, preferred_element_type=jnp.float32)  11.7 us
    dot_general x1, matrix products, feed_forward_rows(): gate_proj = jnp.dot(picked, gate_weight, preferred_element_type=jnp.float32)  6.2 us
  transfers between devices with their start and end apart: 2, of which 2 were waited for; matrix products, arithmetic and copies ran while one was open for 0% of the time, Pallas kernels for 0%

commit v1 on v0

v1 whole, which is shorter than its diff:
```python
import functools

import jax
import jax.numpy as jnp
from jax import lax
from jax.experimental import pallas as pl
from jax.experimental.pallas import tpu as pltpu
from jax.sharding import PartitionSpec as P

HEADS = 32
KVH = 4
HD = 128


rope_base = 500000.0
norm_epsilon = 1e-05

MESH = pl.DeviceIdType.MESH
UP, DOWN, SIDE, CORE = range(4)


def rotate_heads(values, angles):
    middle = values.shape[-1] // 2
    cosine = jnp.cos(angles)
    sine = jnp.sin(angles)
    first = values[..., :middle]
    second = values[..., middle:]
    return jnp.concatenate(
        [first * cosine - second * sine, second * cosine + first * sine], axis=-1
    )


def attend_kernel(
    C, lengths_ref, q_ref, dk_ref, dv_ref, k_ref, v_ref, residual_ref, gain_ref,
    stream_ref, normed_ref, mixed_ref,
):
    r = pl.program_id(0)
    requests = pl.num_programs(0)
    slots = k_ref.shape[1]
    group = HEADS // KVH
    q = q_ref[0]
    scale = HD ** (-0.5)
    scores = jnp.concatenate(
        [
            lax.dot_general(
                q[g * 2 * group : (g + 1) * 2 * group],
                k_ref[0, :, g * HD : (g + 1) * HD],
                (((1,), (1,)), ((), ())),
                preferred_element_type=jnp.float32,
            )
            for g in range(KVH)
        ],
        axis=0,
    ) * scale
    rows = 2 * HEADS
    inside = lax.broadcasted_iota(jnp.int32, (rows, slots), 1) < lengths_ref[r]
    scores = jnp.where(inside, scores, -jnp.inf)

    def spread(ref, t):
        part = ref[0, t].astype(jnp.float32)
        return jnp.concatenate(
            [jnp.broadcast_to(part[g : g + 1], (2 * group, HD)) for g in range(KVH)], axis=0
        )

    wide = q.astype(jnp.float32)
    first = jnp.sum(wide * spread(dk_ref, 0), axis=-1, keepdims=True) * scale
    second = jnp.sum(wide * spread(dk_ref, 1), axis=-1, keepdims=True) * scale
    late = (lax.broadcasted_iota(jnp.int32, (rows, 1), 0) // group) % 2 == 1
    second = jnp.where(late, second, -jnp.inf)
    highest = jnp.maximum(jnp.max(scores, axis=-1, keepdims=True), jnp.maximum(first, second))
    scores = jnp.exp(scores - highest)
    first = jnp.exp(first - highest)
    second = jnp.exp(second - highest)
    total = jnp.sum(scores, axis=-1, keepdims=True) + first + second
    weights = (scores / total).astype(jnp.bfloat16)
    first = (first / total).astype(jnp.bfloat16).astype(jnp.float32)
    second = (second / total).astype(jnp.bfloat16).astype(jnp.float32)
    extra = first * spread(dv_ref, 0) + second * spread(dv_ref, 1)
    for g in range(KVH):
        at = slice(g * 2 * group, (g + 1) * 2 * group)
        mixed = extra[at] + jnp.dot(
            weights[at], v_ref[0, :, g * HD : (g + 1) * HD], preferred_element_type=jnp.float32
        )
        for s in range(2):
            start = pl.multiple_of((r * 2 + s) * HEADS, 8) + g * group
            mixed_ref[pl.ds(start, group), :] = mixed[s * group : (s + 1) * group]

    @pl.when(r == requests - 1)
    def _():
        count = residual_ref.shape[0]
        square = jnp.zeros((count, HD), jnp.float32)
        for h in range(HEADS):
            at = slice(h * HD, (h + 1) * HD)
            value = residual_ref[:, at].astype(jnp.float32) + mixed_ref[pl.ds(h, count, stride=HEADS), :]
            value = value.astype(jnp.bfloat16)
            stream_ref[:, at] = value
            value = value.astype(jnp.float32)
            square += value * value
        mean = jnp.sum(square, axis=-1, keepdims=True) / (HEADS * HD)
        factor = lax.rsqrt(mean + norm_epsilon)
        width = normed_ref.shape[2]
        for k in range(C):
            at = slice(k * width, (k + 1) * width)
            normed_ref[k] = (
                stream_ref[:, at].astype(jnp.float32) * factor * gain_ref[:, at].astype(jnp.float32)
            ).astype(jnp.bfloat16)


def attend(C, queries, new_keys, new_values, key_cache, value_cache, residual, gain, lengths, positions):
    requests, drafts = queries.shape[:2]
    slots = key_cache.shape[1]
    group = HEADS // KVH
    frequency = rope_base ** (-2.0 * jnp.arange(HD // 2, dtype=jnp.float32) / HD)
    offsets = (
        positions.astype(jnp.float32)[:, None] + jnp.arange(drafts, dtype=jnp.float32)[None, :]
    )
    angles = offsets[:, :, None, None] * frequency
    q = rotate_heads(queries.astype(jnp.float32).reshape(requests, drafts, HEADS, HD), angles)
    q = q.astype(jnp.bfloat16).reshape(requests, drafts, KVH, group, HD)
    q = q.transpose(0, 2, 1, 3, 4).reshape(requests, KVH * drafts * group, HD)
    dk = rotate_heads(new_keys.astype(jnp.float32).reshape(requests, drafts, KVH, HD), angles)
    dk = dk.astype(jnp.bfloat16)
    dv = new_values.reshape(requests, drafts, KVH, HD)
    count = requests * drafts
    width = HEADS * HD
    return pl.pallas_call(
        functools.partial(attend_kernel, C),
        grid=(requests,),
        in_specs=[
            pl.BlockSpec(memory_space=pltpu.SMEM),
            pl.BlockSpec((1, 2 * HEADS, HD), lambda r: (r, 0, 0)),
            pl.BlockSpec((1, drafts, KVH, HD), lambda r: (r, 0, 0, 0)),
            pl.BlockSpec((1, drafts, KVH, HD), lambda r: (r, 0, 0, 0)),
            pl.BlockSpec((1, slots, KVH * HD), lambda r: (r, 0, 0)),
            pl.BlockSpec((1, slots, KVH * HD), lambda r: (r, 0, 0)),
            pl.BlockSpec((count, width), lambda r: (0, 0)),
            pl.BlockSpec((1, width), lambda r: (0, 0)),
        ],
        out_specs=[
            pl.BlockSpec((count, width), lambda r: (0, 0)),
            pl.BlockSpec((C, count, width // C), lambda r: (0, 0, 0)),
        ],
        out_shape=[
            jax.ShapeDtypeStruct((count, width), jnp.bfloat16),
            jax.ShapeDtypeStruct((C, count, width // C), jnp.bfloat16),
        ],
        scratch_shapes=[pltpu.VMEM((count * HEADS, HD), jnp.float32)],
        cost_estimate=pl.CostEstimate(flops=10**8, bytes_accessed=5 * 10**6, transcendentals=10**5),
    )(lengths, q, dk, dv, key_cache, value_cache, residual, gain)


def feed_kernel(
    C, Z, Y, normed_ref, stream_ref, wg_hbm, wu_hbm, wd_hbm, out_ref,
    gath, wg, wu, wd, acc_g, acc_u, hid, part, r_core, r_side, r_line, fin,
    w_sem, ag_send, ag_recv, core_send, core_recv, side_send, side_recv, line_send, line_recv,
):
    c = lax.axis_index("attn")
    f = lax.axis_index("ffn")
    z, y = f // Y, f % Y
    R = stream_ref.shape[0]
    N = 2 * Y * Z
    kc = gath.shape[2]
    width = part.shape[2]
    up = {"ffn": (z + 1) * Y + y}
    down = {"ffn": (z - 1) * Y + y}
    side = {"ffn": z * Y + (Y - 1 - y)}
    core = {"attn": 1 - c}
    targets = [up, down, side, core]
    has_up, has_down = z < Z - 1, z > 0

    weight_copies = []
    for k in range(C):
        at = pl.ds(k * kc, kc)
        weight_copies.append(pltpu.make_async_copy(wg_hbm.at[at, :], wg.at[at, :], w_sem.at[0, k]))
        weight_copies.append(pltpu.make_async_copy(wu_hbm.at[at, :], wu.at[at, :], w_sem.at[1, k]))
    for n in range(C):
        at = pl.ds(n * width, width)
        weight_copies.append(pltpu.make_async_copy(wd_hbm.at[:, at], wd.at[:, at], w_sem.at[2, n]))
    for copy in weight_copies:
        copy.start()

    barrier = pltpu.get_barrier_semaphore()

    def greet(target):
        pl.semaphore_signal(barrier, inc=1, device_id=target, device_id_type=MESH)

    greet(core)
    if Y == 2:
        greet(side)
    pl.when(has_up)(lambda: greet(up))
    pl.when(has_down)(lambda: greet(down))

    def index(cc, yy, zz):
        return (cc * Y + yy) * Z + zz

    def rows(at, count=1):
        return pl.ds(pl.multiple_of(at * R, R), count * R)

    own = index(c, y, z)
    for k in range(C):
        gath[k, rows(own), :] = normed_ref[k]

    peers = 2 if Y == 2 else 1
    ends = jnp.logical_or(z == 0, z == Z - 1)
    pl.when(ends)(lambda: pl.semaphore_wait(barrier, peers + 1))
    pl.when(jnp.logical_not(ends))(lambda: pl.semaphore_wait(barrier, peers + 2))

    def ag(k, block, way):
        at = gath.at[k, rows(block), :]
        return pltpu.make_async_remote_copy(
            src_ref=at, dst_ref=at, send_sem=ag_send.at[way, k, block],
            recv_sem=ag_recv.at[k, block], device_id=targets[way], device_id_type=MESH,
        )

    def line_step(d, k, act):
        if d == 0:
            pl.when(has_up)(lambda: act(k, own, UP))
            pl.when(has_down)(lambda: act(k, own, DOWN))
            if Y == 2:
                act(k, own, SIDE)
            act(k, own, CORE)
            return

        def arrived(block, way, more):
            if act is start:
                ag(k, block, way).wait_recv()
            pl.when(more)(lambda: act(k, block, way))
            if Y == 2:
                act(k, block, SIDE)
            act(k, block, CORE)

        pl.when(z - d >= 0)(lambda: arrived(index(c, y, z - d), UP, has_up))
        pl.when(z + d < Z)(lambda: arrived(index(c, y, z + d), DOWN, has_down))

    def side_step(d, k, act):
        def arrived(block):
            if act is start:
                ag(k, block, SIDE).wait_recv()
            act(k, block, CORE)

        if d == 0:
            arrived(index(c, 1 - y, z))
        else:
            pl.when(z - d >= 0)(lambda: arrived(index(c, 1 - y, z - d)))
            pl.when(z + d < Z)(lambda: arrived(index(c, 1 - y, z + d)))

    def start(k, block, way):
        ag(k, block, way).start()

    def finish(k, block, way):
        ag(k, block, way).wait_send()

    def project(k):
        for j in range(Y * Z):
            ag(k, (1 - c) * Y * Z + j, CORE).wait_recv()
        weight_copies[2 * k].wait()
        weight_copies[2 * k + 1].wait()
        at = pl.ds(k * kc, kc)
        ff = wg.shape[1]
        x = gath[k]
        if ff % 128 == 0:
            both = jnp.concatenate([wg[at, :], wu[at, :]], axis=1)
            both = jnp.dot(x, both, preferred_element_type=jnp.float32)
            new_g, new_u = both[:, :ff], both[:, ff:]
        else:
            new_g = jnp.dot(x, wg[at, :], preferred_element_type=jnp.float32)
            new_u = jnp.dot(x, wu[at, :], preferred_element_type=jnp.float32)
        if k > 0:
            new_g = acc_g[...] + new_g
            new_u = acc_u[...] + new_u
        if k < C - 1:
            acc_g[...] = new_g
            acc_u[...] = new_u
        else:
            hid[...] = (new_g / (1.0 + jnp.exp(-new_g)) * new_u).astype(jnp.bfloat16)

    lag = 2
    for t in range(C + Z + lag):
        for d in range(Z):
            if 0 <= t - d < C:
                line_step(d, t - d, start)
        if Y == 2:
            for d in range(Z):
                if 0 <= t - lag - d < C:
                    side_step(d, t - lag - d, start)
        k = t - lag - (Z - 1)
        if 0 <= k < C:
            project(k)

    half = Y * Z

    def core_copy(n):
        return pltpu.make_async_remote_copy(
            src_ref=part.at[n, rows((1 - c) * half, half), :], dst_ref=r_core.at[n],
            send_sem=core_send.at[n], recv_sem=core_recv.at[n],
            device_id=core, device_id_type=MESH,
        )

    def side_copy(n):
        return pltpu.make_async_remote_copy(
            src_ref=part.at[n, rows(index(c, 1 - y, 0), Z), :], dst_ref=r_side.at[n],
            send_sem=side_send.at[n], recv_sem=side_recv.at[n],
            device_id=side, device_id_type=MESH,
        )

    def line_copy(n, goal, way):
        slot = goal + 1 if way == UP else goal
        return pltpu.make_async_remote_copy(
            src_ref=part.at[n, rows(index(c, y, goal)), :], dst_ref=r_line.at[n, rows(slot), :],
            send_sem=line_send.at[n, goal], recv_sem=line_recv.at[n, slot],
            device_id=targets[way], device_id_type=MESH,
        )

    def add(n, at, other):
        part[n, at, :] = (
            part[n, at, :].astype(jnp.float32) + other.astype(jnp.float32)
        ).astype(jnp.bfloat16)

    def produce(n):
        weight_copies[2 * C + n].wait()
        at = pl.ds(n * width, width)
        part[n] = jnp.dot(
            hid[...], wd[:, at], preferred_element_type=jnp.float32
        ).astype(jnp.bfloat16)
        core_copy(n).start()

    def after_core(n):
        core_copy(n).wait_recv()
        if Y == 2:
            add(n, rows(index(c, 1 - y, 0), Z), r_core[n, rows((1 - y) * Z, Z), :])
            side_copy(n).start()
        add(n, rows(index(c, y, 0), Z), r_core[n, rows(y * Z, Z), :])

    def after_side(n):
        if Y == 2:
            side_copy(n).wait_recv()
            add(n, rows(index(c, y, 0), Z), r_side[n])

    def along(n, way):
        source = has_down if way == UP else has_up
        for step in range(Z - 1):
            goal = Z - 1 - step if way == UP else step

            def move(goal=goal):
                @pl.when(source)
                def _():
                    line_copy(n, goal, way).wait_recv()
                    slot = goal + 1 if way == UP else goal
                    add(n, rows(index(c, y, goal)), r_line[n, rows(slot), :])

                line_copy(n, goal, way).start()

            pl.when(goal > z if way == UP else goal < z)(move)

    def complete(n):
        at = pl.ds(n * width, width)
        fin[...] = part[n, rows(own), :].astype(jnp.float32)

        @pl.when(has_down)
        def _():
            line_copy(n, z, UP).wait_recv()
            fin[...] += r_line[n, rows(z + 1), :].astype(jnp.float32)

        @pl.when(has_up)
        def _():
            line_copy(n, z, DOWN).wait_recv()
            fin[...] += r_line[n, rows(z), :].astype(jnp.float32)

        out_ref[:, at] = (stream_ref[:, at].astype(jnp.float32) + fin[...]).astype(jnp.bfloat16)

    if C == 1:
        produce(0)
        after_core(0)
        after_side(0)
        along(0, UP)
        along(0, DOWN)
        complete(0)
    else:
        for t in range(C + Z + 4):
            if t < C:
                produce(t)
            if 0 <= t - 1 < C:
                after_core(t - 1)
            if 0 <= t - 2 < C:
                after_side(t - 2)
            for hop in range(Z - 1):
                n = t - 2 - hop
                if 0 <= n < C:
                    pl.when(z == hop)(functools.partial(along, n, UP))
                    pl.when(z == Z - 1 - hop)(functools.partial(along, n, DOWN))
            if 0 <= t - 2 - Z < C:
                complete(t - 2 - Z)

    for k in range(C):
        for d in range(Z):
            line_step(d, k, finish)
            if Y == 2:
                side_step(d, k, finish)
        core_copy(k).wait_send()
        if Y == 2:
            side_copy(k).wait_send()
        for goal in range(Z):
            pl.when(goal > z)(lambda goal=goal: line_copy(k, goal, UP).wait_send())
            pl.when(goal < z)(lambda goal=goal: line_copy(k, goal, DOWN).wait_send())


def feed(C, Z, Y, normed, stream, wg, wu, wd):
    R, D = stream.shape
    ff = wg.shape[1]
    N = 2 * Y * Z
    M = N * R
    width = D // C
    bf16 = jnp.bfloat16
    dma = pltpu.SemaphoreType.DMA
    vmem = pl.BlockSpec(memory_space=pltpu.VMEM)
    hbm = pl.BlockSpec(memory_space=pl.ANY)
    return pl.pallas_call(
        functools.partial(feed_kernel, C, Z, Y),
        out_shape=jax.ShapeDtypeStruct((R, D), bf16),
        in_specs=[vmem, vmem, hbm, hbm, hbm],
        out_specs=vmem,
        scratch_shapes=[
            pltpu.VMEM((C, M, width), bf16),
            pltpu.VMEM((D, ff), bf16),
            pltpu.VMEM((D, ff), bf16),
            pltpu.VMEM((ff, D), bf16),
            pltpu.VMEM((M, ff), jnp.float32),
            pltpu.VMEM((M, ff), jnp.float32),
            pltpu.VMEM((M, ff), bf16),
            pltpu.VMEM((C, M, width), bf16),
            pltpu.VMEM((C, M // 2, width), bf16),
            pltpu.VMEM((C, Z * R, width), bf16),
            pltpu.VMEM((C, (Z + 1) * R, width), bf16),
            pltpu.VMEM((R, width), jnp.float32),
            dma((3, C)),
            dma((4, C, N)),
            dma((C, N)),
            dma((C,)),
            dma((C,)),
            dma((C,)),
            dma((C,)),
            dma((C, Z)),
            dma((C, Z + 1)),
        ],
        compiler_params=pltpu.CompilerParams(
            collective_id=0, has_side_effects=True, vmem_limit_bytes=58 * 1024 * 1024
        ),
        cost_estimate=pl.CostEstimate(
            flops=6 * M * D * ff, bytes_accessed=6 * D * ff, transcendentals=M * ff
        ),
    )(normed, stream, wg, wu, wd)


def shards(
    Z,
    Y,
    C,
    queries,
    new_keys,
    new_values,
    key_cache,
    value_cache,
    residual_in,
    norm_gain,
    gate_weight,
    up_weight,
    down_weight,
    live_counts,
    cache_lengths,
    positions,
):
    requests, drafts, width = residual_in.shape
    stream, normed = attend(
        C, queries, new_keys, new_values, key_cache, value_cache,
        residual_in.reshape(requests * drafts, width), norm_gain.reshape(1, width),
        cache_lengths, positions,
    )
    combined = feed(C, Z, Y, normed, stream, gate_weight, up_weight, down_weight)
    combined = combined.reshape(requests, drafts, width)
    live_slot = jnp.arange(requests) < live_counts[0]
    return jnp.where(live_slot[:, None, None], combined, jnp.zeros_like(combined))


def solution(mesh):
    ffn = mesh.shape["ffn"]
    Y = 2 if ffn % 2 == 0 and ffn <= 8 else 1
    C = 4 if ffn <= 8 else 1
    return jax.shard_map(
        functools.partial(shards, ffn // Y, Y, C),
        mesh=mesh,
        in_specs=(
            P(("rep", "attn", "ffn"), None, None),
            P(("rep", "attn", "ffn"), None, None),
            P(("rep", "attn", "ffn"), None, None),
            P(("rep", "attn", "ffn"), None, None),
            P(("rep", "attn", "ffn"), None, None),
            P(("rep", "attn", "ffn"), None, None),
            P(),
            P(None, ("attn", "ffn")),
            P(None, ("attn", "ffn")),
            P(("attn", "ffn"), None),
            P(("rep", "attn", "ffn")),
            P(("rep", "attn", "ffn")),
            P(("rep", "attn", "ffn")),
        ),
        out_specs=P(("rep", "attn", "ffn"), None, None),
        check_vma=False,
    )
```

time: 162 us -> 75.2 us (0.46)
  waiting for transfers between devices: 115 us -> 0 us
  Pallas kernels: 0 us -> 63.5 us
  matrix products: 20.1 us -> 0 us
  between operations: 14.2 us -> 0.71 us
  local copies, waits for them, and re-layouts: 9.28 us -> 7.65 us
    reduce_scatter x1 -> x0, waiting for transfers between devices: 70.6 us -> none  [shards(): lax.psum_scatter(compute(jnp.int32(0), requests * drafts * lax.axis_size(...]
    pallas_call x0 -> x2, Pallas kernels: none -> 63.5 us  [the longest x1 55.6 us: feed(): pl.pallas_call(functools.partial(feed_kernel, C, Z, Y), out_shape=jax.Sha...]
    all_gather x1 -> x0, waiting for transfers between devices: 44.2 us -> none  [shards(): gathered = lax.all_gather(normed, ('attn', 'ffn'), axis=0, tiled=True)]
    dot_general x6 -> x0, matrix products: 20.1 us -> none  [the longest x1 11.7 us: feed_forward_rows(): return jnp.dot(hidden, down_weight, preferred_element_type=jnp.float32)]
  transfers between devices with their start and end apart: 2 -> 0, of which waited for: 2 -> 0; matrix products, arithmetic and copies ran while one was open for 0% -> 0% of each run, Pallas kernels for 0% -> 0%
where the time goes in v1:
time: 75.2 us; the launch traced here: 74.7 us
  Pallas kernels  63.5 us (84%)
  local copies, waits for them, and re-layouts  7.65 us (10%)
  other arithmetic  2.82 us (4%)
    pallas_call x1, Pallas kernels, feed(): pl.pallas_call(functools.partial(feed_kernel, C, Z, Y), out_shape=jax.Sha...  55.6 us
    pallas_call x1, Pallas kernels, attend(): pl.pallas_call(functools.partial(attend_kernel, C), grid=(requests,), in_...  7.88 us
    reshape x1, local copies, waits for them, and re-layouts, shards(): residual_in.reshape(requests * drafts, width)  1.61 us

profile of v1, /device:TPU:0, one launch (start us, length us, event | category | flops | bytes accessed | tf_op | source)
XLA Modules:
  0.0 74.7 jit_solution(14872769362982849730)
XLA Ops:
  0.0 0.7 convert_element_type.3
  0.7 0.1 iota_add_fusion
  0.7 0.2 multiply_cosine_fusion
  0.9 1.0 %reshape.82 = f32[8,2,32,128]{3,2,1,0:T(8,128)S(1)} reshape(bf16[8,2,4096]{2,1,0:T(2,128)(2,1)} %param.13) | data formatting | bytes 393216 | tf_op jit(solution)/shard_map/reshape | solution.py:118
  1.9 0.2 fusion
  2.1 0.1 maximum_bitcast_fusion
  2.2 0.7 copy.14
  2.9 0.7 reshape.84
  3.6 0.1 subtract_convert_fusion.1
  3.7 0.7 pad_maximum_fusion.dk_ref
  4.4 1.6 %reshape.78.residual_ref = bf16[16,4096]{1,0:T(8,128)(2,1)} reshape(bf16[8,2,4096]{2,1,0:T(2,128)(2,1)} %param.18) | data formatting | bytes 262144 | tf_op jit(solution)/shard_map/reshape | solution.py:475
  6.0 1.3 %reshape.77.dv_ref = bf16[8,2,4,128]{3,2,1,0:T(4,128)(2,1)} reshape(bf16[8,2,512]{2,1,0:T(2,128)(2,1)} %param.15) | data formatting | bytes 32768 | tf_op jit(solution)/shard_map/reshape | solution.py:123
  7.4 1.3 %reshape.79.gain_ref = bf16[1,4096]{1,0:T(2,128)(2,1)} reshape(bf16[4096]{0:T(1024)(128)(2,1)} %param.19) | data formatting | bytes 16384 | tf_op jit(solution)/shard_map/reshape | solution.py:475
  8.7 7.9 %shard_map.127 = (bf16[16,4096]{1,0:T(8,128)(2,1)}, bf16[4,16,1024]{2,1,0:T(8,128)(2,1)}) custom-call(s32[8]{0:T(128)} %lengths_ref.1, bf16[8,64,128]{2,1,0:T(8,128)(2,1)} %bitcast.9, bf16[8,2,4,128]{3,2,1,0:T(4,128)(2,1)} %pad_maximum_fusion.dk_ref, bf16[8,2,4,128]{3,2,1,0:T(4,128)(2,1)} %reshape.77.dv_ref, bf16[8,256,512]{2,1,0:T(8,128)(2,1)} %k_ref.1, ...), custom_call_target="tpu_custom_call" | custom-call | flops 100000000 | bytes 5000000 | tf_op jit(solution)/shard_map/pallas_call | solution.py:126
  16.5 55.6 %shard_map.128 = bf16[16,4096]{1,0:T(8,128)(2,1)} custom-call(bf16[4,16,1024]{2,1,0:T(8,128)(2,1)} %get-tuple-element.7.normed_ref, bf16[16,4096]{1,0:T(8,128)(2,1)} %get-tuple-element.8.stream_ref, bf16[4096,896]{1,0:T(8,128)(2,1)} %wg_hbm.1, bf16[4096,896]{1,0:T(8,128)(2,1)} %wu_hbm.1, bf16[896,4096]{1,0:T(8,128)(2,1)} %wd_hbm.1), custom_call_target="tpu_custom_call" | custom-call | flops 5637144576 | bytes 22020096 | tf_op jit(solution)/shard_map/pallas_call | solution.py:417
  72.2 1.0 %reshape.80 = bf16[8,2,4096]{2,1,0:T(2,128)(2,1)S(1)} reshape(bf16[16,4096]{1,0:T(8,128)(2,1)} %shard_map.128) | data formatting | bytes 262144 | tf_op jit(solution)/shard_map/reshape | solution.py:479
  73.9 0.8 %broadcast_select_fusion = bf16[8,2,4096]{2,1,0:T(2,128)(2,1)} fusion(bf16[8,2,4096]{2,1,0:T(2,128)(2,1)S(1)} %reshape.80, pred[8]{0:T(512)(128)(4,1)S(1)} %iota_compare_fusion), kind=kLoop, calls=%fused_computation.2 | loop fusion | flops 65536 | bytes 262152 | tf_op jit(solution)/shard_map/jit(_where)/select_n | solution.py:481
  (2 shorter events, 0.0 us)

commit v2 on v1

--- a/solution.py
+++ b/solution.py
@@ -19,79 +19,110 @@
 UP, DOWN, SIDE, CORE = range(4)
 
 
-def rotate_heads(values, angles):
-    middle = values.shape[-1] // 2
-    cosine = jnp.cos(angles)
-    sine = jnp.sin(angles)
-    first = values[..., :middle]
-    second = values[..., middle:]
-    return jnp.concatenate(
-        [first * cosine - second * sine, second * cosine + first * sine], axis=-1
-    )
-
-
 def attend_kernel(
-    C, lengths_ref, q_ref, dk_ref, dv_ref, k_ref, v_ref, residual_ref, gain_ref,
-    stream_ref, normed_ref, mixed_ref,
+    C, batch, lengths_ref, q_ref, dk_ref, dv_ref, k_ref, v_ref, residual_ref, gain_ref, cos_ref, sin_ref,
+    stream_ref, normed_ref, wide_ref, heads_ref, mixed_ref,
 ):
-    r = pl.program_id(0)
-    requests = pl.num_programs(0)
+    step = pl.program_id(0)
     slots = k_ref.shape[1]
+    requests = q_ref.shape[0]
+    count = 2 * requests
     group = HEADS // KVH
-    q = q_ref[0]
     scale = HD ** (-0.5)
-    scores = jnp.concatenate(
-        [
-            lax.dot_general(
-                q[g * 2 * group : (g + 1) * 2 * group],
-                k_ref[0, :, g * HD : (g + 1) * HD],
-                (((1,), (1,)), ((), ())),
-                preferred_element_type=jnp.float32,
+    rows = 2 * HEADS
+
+    def widen(ref):
+        for r in range(requests):
+            wide_ref[2 * r : 2 * r + 2, :] = ref[r].astype(jnp.float32)
+
+    def rotate(value, cosine, sine):
+        return value * cosine + pltpu.roll(value, HD // 2, 1) * sine
+
+    @pl.when(step == 0)
+    def _():
+        widen(q_ref)
+        for h in range(HEADS):
+            value = rotate(wide_ref[:, h * HD : (h + 1) * HD], cos_ref[...], sin_ref[...])
+            heads_ref[pl.ds(h, count, stride=HEADS), :] = value
+        widen(residual_ref)
+
+    late = (lax.broadcasted_iota(jnp.int32, (rows, 1), 0) // group) % 2 == 1
+    column = lax.broadcasted_iota(jnp.int32, (rows, slots), 1)
+
+    def spread(part, t):
+        return jnp.concatenate(
+            [
+                jnp.broadcast_to(part[t : t + 1, g * HD : (g + 1) * HD], (2 * group, HD))
+                for g in range(KVH)
+            ],
+            axis=0,
+        )
+
+    picked = []
+    for b in range(batch):
+        r = step * batch + b
+        first_row = pl.multiple_of(r * rows, 8)
+        q = jnp.concatenate(
+            [
+                heads_ref[pl.ds(first_row + s * HEADS + g * group, group), :]
+                for g in range(KVH)
+                for s in range(2)
+            ],
+            axis=0,
+        ).astype(jnp.bfloat16)
+        scores = jnp.concatenate(
+            [
+                lax.dot_general(
+                    q[g * 2 * group : (g + 1) * 2 * group],
+                    k_ref[b, :, g * HD : (g + 1) * HD],
+                    (((1,), (1,)), ((), ())),
+                    preferred_element_type=jnp.float32,
+                )
+                for g in range(KVH)
+            ],
+            axis=0,
+        ) * scale
+        scores = jnp.where(column < lengths_ref[r], scores, -jnp.inf)
+        cosine, sine = cos_ref[pl.ds(2 * r, 2), :], sin_ref[pl.ds(2 * r, 2), :]
+        fresh = dk_ref[b].astype(jnp.float32)
+        fresh = jnp.concatenate(
+            [rotate(fresh[:, g * HD : (g + 1) * HD], cosine, sine) for g in range(KVH)], axis=1
+        ).astype(jnp.bfloat16).astype(jnp.float32)
+        wide = q.astype(jnp.float32)
+        first = jnp.sum(wide * spread(fresh, 0), axis=-1, keepdims=True) * scale
+        second = jnp.sum(wide * spread(fresh, 1), axis=-1, keepdims=True) * scale
+        second = jnp.where(late, second, -jnp.inf)
+        picked.append((r, scores, first, second))
+
+    for b in range(batch):
+        r, scores, first, second = picked[b]
+        highest = jnp.maximum(jnp.max(scores, axis=-1, keepdims=True), jnp.maximum(first, second))
+        scores = jnp.exp(scores - highest)
+        first = jnp.exp(first - highest)
+        second = jnp.exp(second - highest)
+        total = 1.0 / (jnp.sum(scores, axis=-1, keepdims=True) + first + second)
+        weights = (scores * total).astype(jnp.bfloat16)
+        first = (first * total).astype(jnp.bfloat16).astype(jnp.float32)
+        second = (second * total).astype(jnp.bfloat16).astype(jnp.float32)
+        fresh = dv_ref[b].astype(jnp.float32)
+        extra = first * spread(fresh, 0) + second * spread(fresh, 1)
+        first_row = pl.multiple_of(r * rows, 8)
+        for g in range(KVH):
+            at = slice(g * 2 * group, (g + 1) * 2 * group)
+            mixed = extra[at] + jnp.dot(
+                weights[at], v_ref[b, :, g * HD : (g + 1) * HD], preferred_element_type=jnp.float32
             )
-            for g in range(KVH)
-        ],
-        axis=0,
-    ) * scale
-    rows = 2 * HEADS
-    inside = lax.broadcasted_iota(jnp.int32, (rows, slots), 1) < lengths_ref[r]
-    scores = jnp.where(inside, scores, -jnp.inf)
-
-    def spread(ref, t):
-        part = ref[0, t].astype(jnp.float32)
-        return jnp.concatenate(
-            [jnp.broadcast_to(part[g : g + 1], (2 * group, HD)) for g in range(KVH)], axis=0
-        )
-
-    wide = q.astype(jnp.float32)
-    first = jnp.sum(wide * spread(dk_ref, 0), axis=-1, keepdims=True) * scale
-    second = jnp.sum(wide * spread(dk_ref, 1), axis=-1, keepdims=True) * scale
-    late = (lax.broadcasted_iota(jnp.int32, (rows, 1), 0) // group) % 2 == 1
-    second = jnp.where(late, second, -jnp.inf)
-    highest = jnp.maximum(jnp.max(scores, axis=-1, keepdims=True), jnp.maximum(first, second))
-    scores = jnp.exp(scores - highest)
-    first = jnp.exp(first - highest)
-    second = jnp.exp(second - highest)
-    total = jnp.sum(scores, axis=-1, keepdims=True) + first + second
-    weights = (scores / total).astype(jnp.bfloat16)
-    first = (first / total).astype(jnp.bfloat16).astype(jnp.float32)
-    second = (second / total).astype(jnp.bfloat16).astype(jnp.float32)
-    extra = first * spread(dv_ref, 0) + second * spread(dv_ref, 1)
-    for g in range(KVH):
-        at = slice(g * 2 * group, (g + 1) * 2 * group)
-        mixed = extra[at] + jnp.dot(
-            weights[at], v_ref[0, :, g * HD : (g + 1) * HD], preferred_element_type=jnp.float32
-        )
-        for s in range(2):
-            start = pl.multiple_of((r * 2 + s) * HEADS, 8) + g * group
-            mixed_ref[pl.ds(start, group), :] = mixed[s * group : (s + 1) * group]
-
-    @pl.when(r == requests - 1)
+            for s in range(2):
+                mixed_ref[pl.ds(first_row + s * HEADS + g * group, group), :] = mixed[
+                    s * group : (s + 1) * group
+                ]
+
+    @pl.when(step == pl.num_programs(0) - 1)
     def _():
-        count = residual_ref.shape[0]
         square = jnp.zeros((count, HD), jnp.float32)
         for h in range(HEADS):
             at = slice(h * HD, (h + 1) * HD)
-            value = residual_ref[:, at].astype(jnp.float32) + mixed_ref[pl.ds(h, count, stride=HEADS), :]
+            value = wide_ref[:, at] + mixed_ref[pl.ds(h, count, stride=HEADS), :]
             value = value.astype(jnp.bfloat16)
             stream_ref[:, at] = value
             value = value.astype(jnp.float32)
@@ -102,39 +133,38 @@
         for k in range(C):
             at = slice(k * width, (k + 1) * width)
             normed_ref[k] = (
-                stream_ref[:, at].astype(jnp.float32) * factor * gain_ref[:, at].astype(jnp.float32)
+                stream_ref[:, at].astype(jnp.float32) * factor * gain_ref[at].astype(jnp.float32)[None, :]
             ).astype(jnp.bfloat16)
 
 
 def attend(C, queries, new_keys, new_values, key_cache, value_cache, residual, gain, lengths, positions):
     requests, drafts = queries.shape[:2]
     slots = key_cache.shape[1]
-    group = HEADS // KVH
-    frequency = rope_base ** (-2.0 * jnp.arange(HD // 2, dtype=jnp.float32) / HD)
-    offsets = (
-        positions.astype(jnp.float32)[:, None] + jnp.arange(drafts, dtype=jnp.float32)[None, :]
-    )
-    angles = offsets[:, :, None, None] * frequency
-    q = rotate_heads(queries.astype(jnp.float32).reshape(requests, drafts, HEADS, HD), angles)
-    q = q.astype(jnp.bfloat16).reshape(requests, drafts, KVH, group, HD)
-    q = q.transpose(0, 2, 1, 3, 4).reshape(requests, KVH * drafts * group, HD)
-    dk = rotate_heads(new_keys.astype(jnp.float32).reshape(requests, drafts, KVH, HD), angles)
-    dk = dk.astype(jnp.bfloat16)
-    dv = new_values.reshape(requests, drafts, KVH, HD)
     count = requests * drafts
     width = HEADS * HD
+    batch = 4 if requests % 4 == 0 else 1
+    place = jnp.arange(HD)
+    frequency = rope_base ** (-2.0 * (place % (HD // 2)).astype(jnp.float32) / HD)
+    row = jnp.arange(count)
+    offsets = jnp.repeat(positions, drafts).astype(jnp.float32) + (row % drafts).astype(jnp.float32)
+    angles = offsets[:, None] * frequency[None, :]
+    cosine = jnp.cos(angles)
+    sine = jnp.where(place[None, :] < HD // 2, -jnp.sin(angles), jnp.sin(angles))
+    whole = pl.BlockSpec(memory_space=pltpu.VMEM)
     return pl.pallas_call(
-        functools.partial(attend_kernel, C),
-        grid=(requests,),
+        functools.partial(attend_kernel, C, batch),
+        grid=(requests // batch,),
         in_specs=[
             pl.BlockSpec(memory_space=pltpu.SMEM),
-            pl.BlockSpec((1, 2 * HEADS, HD), lambda r: (r, 0, 0)),
-            pl.BlockSpec((1, drafts, KVH, HD), lambda r: (r, 0, 0, 0)),
-            pl.BlockSpec((1, drafts, KVH, HD), lambda r: (r, 0, 0, 0)),
-            pl.BlockSpec((1, slots, KVH * HD), lambda r: (r, 0, 0)),
-            pl.BlockSpec((1, slots, KVH * HD), lambda r: (r, 0, 0)),
-            pl.BlockSpec((count, width), lambda r: (0, 0)),
-            pl.BlockSpec((1, width), lambda r: (0, 0)),
+            whole,
+            pl.BlockSpec((batch, drafts, KVH * HD), lambda r: (r, 0, 0)),
+            pl.BlockSpec((batch, drafts, KVH * HD), lambda r: (r, 0, 0)),
+            pl.BlockSpec((batch, slots, KVH * HD), lambda r: (r, 0, 0)),
+            pl.BlockSpec((batch, slots, KVH * HD), lambda r: (r, 0, 0)),
+            whole,
+            whole,
+            whole,
+            whole,
         ],
         out_specs=[
             pl.BlockSpec((count, width), lambda r: (0, 0)),
@@ -144,9 +174,14 @@
             jax.ShapeDtypeStruct((count, width), jnp.bfloat16),
             jax.ShapeDtypeStruct((C, count, width // C), jnp.bfloat16),
         ],
-        scratch_shapes=[pltpu.VMEM((count * HEADS, HD), jnp.float32)],
+        scratch_shapes=[
+            pltpu.VMEM((count, width), jnp.float32),
+            pltpu.VMEM((count * HEADS, HD), jnp.float32),
+            pltpu.VMEM((count * HEADS, HD), jnp.float32),
+        ],
+        compiler_params=pltpu.CompilerParams(vmem_limit_bytes=32 * 1024 * 1024),
         cost_estimate=pl.CostEstimate(flops=10**8, bytes_accessed=5 * 10**6, transcendentals=10**5),
-    )(lengths, q, dk, dv, key_cache, value_cache, residual, gain)
+    )(lengths, queries, new_keys, new_values, key_cache, value_cache, residual, gain, cosine, sine)
 
 
 def feed_kernel(
@@ -366,7 +401,10 @@
             line_copy(n, z, DOWN).wait_recv()
             fin[...] += r_line[n, rows(z), :].astype(jnp.float32)
 
-        out_ref[:, at] = (stream_ref[:, at].astype(jnp.float32) + fin[...]).astype(jnp.bfloat16)
+        fin[...] += stream_ref[:, at].astype(jnp.float32)
+        drafts = out_ref.shape[1]
+        for r in range(out_ref.shape[0]):
+            out_ref[r, :, at] = fin[r * drafts : (r + 1) * drafts, :].astype(jnp.bfloat16)
 
     if C == 1:
         produce(0)
@@ -404,7 +442,7 @@
             pl.when(goal < z)(lambda goal=goal: line_copy(k, goal, DOWN).wait_send())
 
 
-def feed(C, Z, Y, normed, stream, wg, wu, wd):
+def feed(C, Z, Y, shape, normed, stream, wg, wu, wd):
     R, D = stream.shape
     ff = wg.shape[1]
     N = 2 * Y * Z
@@ -416,7 +454,7 @@
     hbm = pl.BlockSpec(memory_space=pl.ANY)
     return pl.pallas_call(
         functools.partial(feed_kernel, C, Z, Y),
-        out_shape=jax.ShapeDtypeStruct((R, D), bf16),
+        out_shape=jax.ShapeDtypeStruct(shape, bf16),
         in_specs=[vmem, vmem, hbm, hbm, hbm],
         out_specs=vmem,
         scratch_shapes=[
@@ -469,14 +507,13 @@
     cache_lengths,
     positions,
 ):
-    requests, drafts, width = residual_in.shape
+    requests = residual_in.shape[0]
     stream, normed = attend(
         C, queries, new_keys, new_values, key_cache, value_cache,
-        residual_in.reshape(requests * drafts, width), norm_gain.reshape(1, width),
+        residual_in, norm_gain,
         cache_lengths, positions,
     )
-    combined = feed(C, Z, Y, normed, stream, gate_weight, up_weight, down_weight)
-    combined = combined.reshape(requests, drafts, width)
+    combined = feed(C, Z, Y, residual_in.shape, normed, stream, gate_weight, up_weight, down_weight)
     live_slot = jnp.arange(requests) < live_counts[0]
     return jnp.where(live_slot[:, None, None], combined, jnp.zeros_like(combined))
 

time: 75.2 us -> 71.2 us (0.947)
  Pallas kernels: 63.5 us -> 58.3 us
  local copies, waits for them, and re-layouts: 7.65 us -> 9.21 us
    unnamed x0 -> x20, local copies, waits for them, and re-layouts: none -> 9.05 us
    reshape x6 -> x0, local copies, waits for them, and re-layouts: 6.97 us -> none  [the longest x1 1.61 us: shards(): residual_in.reshape(requests * drafts, width)]
    pallas_call x1, Pallas kernels: 7.88 us -> 2.65 us  [attend(): pl.pallas_call(functools.partial(attend_kernel, C, batch), grid=(requests...]
    select_n x1, other arithmetic: 0.84 us -> 1.74 us  [shards(): jnp.where(live_slot[:, None, None], combined, jnp.zeros_like(combined))]
    concatenate x2 -> x0, other arithmetic: 0.84 us -> none  [rotate_heads(): jnp.concatenate([first * cosine - second * sine, second * cosine + first...]
where the time goes in v2:
time: 71.2 us; the launch traced here: 70.8 us
  Pallas kernels  58.3 us (82%)
  local copies, waits for them, and re-layouts  9.21 us (13%)
  other arithmetic  2.55 us (4%)
    pallas_call x1, Pallas kernels, feed(): pl.pallas_call(functools.partial(feed_kernel, C, Z, Y), out_shape=jax.Sha...  55.7 us
    unnamed x20, local copies, waits for them, and re-layouts  9.05 us
    pallas_call x1, Pallas kernels, attend(): pl.pallas_call(functools.partial(attend_kernel, C, batch), grid=(requests...  2.65 us
    select_n x1, other arithmetic, shards(): jnp.where(live_slot[:, None, None], combined, jnp.zeros_like(combined))  1.74 us

profile of v2, /device:TPU:0, one launch (start us, length us, event | category | flops | bytes accessed | tf_op | source)
XLA Modules:
  0.0 70.8 jit_solution(9353478459755541132)
XLA Ops:
  0.0 0.7 convert_element_type.25
  0.7 0.1 broadcast_in_dim.27
  0.7 0.1 convert_element_type.26
  0.8 0.1 negate_select_fusion
  1.0 0.0 copy-start
  1.0 1.6 %copy-done = bf16[8,256,512]{2,1,0:T(8,128)(2,1)S(1)} copy-done((bf16[8,256,512]{2,1,0:T(8,128)(2,1)S(1)}, bf16[8,256,512]{2,1,0:T(8,128)(2,1)}, u32[]{:S(2)}) %copy-start) | copy-done | bytes 2097176
  2.6 0.0 copy-start.1
  2.6 1.6 %copy-done.1 = bf16[8,256,512]{2,1,0:T(8,128)(2,1)S(1)} copy-done((bf16[8,256,512]{2,1,0:T(8,128)(2,1)S(1)}, bf16[8,256,512]{2,1,0:T(8,128)(2,1)}, u32[]{:S(2)}) %copy-start.1) | copy-done | bytes 2097176
  4.2 0.0 copy-start.4
  4.2 0.9 %copy-done.4 = bf16[8,2,4096]{2,1,0:T(2,128)(2,1)S(1)} copy-done((bf16[8,2,4096]{2,1,0:T(2,128)(2,1)S(1)}, bf16[8,2,4096]{2,1,0:T(2,128)(2,1)}, u32[]{:S(2)}) %copy-start.4) | copy-done | bytes 131096
  5.1 0.0 copy-start.5
  5.1 0.9 %copy-done.5 = bf16[8,2,4096]{2,1,0:T(2,128)(2,1)S(1)} copy-done((bf16[8,2,4096]{2,1,0:T(2,128)(2,1)S(1)}, bf16[8,2,4096]{2,1,0:T(2,128)(2,1)}, u32[]{:S(2)}) %copy-start.5) | copy-done | bytes 131096
  6.0 0.0 copy-start.6
  6.0 0.7 %copy-done.6 = bf16[8,2,512]{2,1,0:T(2,128)(2,1)S(1)} copy-done((bf16[8,2,512]{2,1,0:T(2,128)(2,1)S(1)}, bf16[8,2,512]{2,1,0:T(2,128)(2,1)}, u32[]{:S(2)}) %copy-start.6) | copy-done | bytes 16408
  6.7 0.0 copy-start.7
  6.7 0.7 %copy-done.7 = bf16[8,2,512]{2,1,0:T(2,128)(2,1)S(1)} copy-done((bf16[8,2,512]{2,1,0:T(2,128)(2,1)S(1)}, bf16[8,2,512]{2,1,0:T(2,128)(2,1)}, u32[]{:S(2)}) %copy-start.7) | copy-done | bytes 16408
  7.4 0.0 copy-start.8
  7.4 0.7 copy-done.8
  8.1 0.0 copy-start.9
  8.1 0.7 copy-done.9
  8.8 2.7 %shard_map.127 = (bf16[16,4096]{1,0:T(8,128)(2,1)S(1)}, bf16[4,16,1024]{2,1,0:T(8,128)(2,1)S(1)}) custom-call(s32[8]{0:T(128)S(1)} %copy-done.9, bf16[8,2,4096]{2,1,0:T(2,128)(2,1)S(1)} %copy-done.4, bf16[8,2,512]{2,1,0:T(2,128)(2,1)S(1)} %copy-done.6, bf16[8,2,512]{2,1,0:T(2,128)(2,1)S(1)} %copy-done.7, bf16[8,256,512]{2,1,0:T(8,128)(2,1)S(1)} %copy-done, ...), custom_call_target="tpu_custom_call" | custom-call | flops 100000000 | bytes 5000000 | tf_op jit(solution)/shard_map/pallas_call | solution.py:154
  11.4 0.0 copy-start.2
  11.4 0.6 copy-done.2
  12.0 0.0 copy-start.3
  12.0 0.7 copy-done.3
  12.7 55.7 %shard_map.128 = bf16[8,2,4096]{2,1,0:T(2,128)(2,1)} custom-call(bf16[4,16,1024]{2,1,0:T(8,128)(2,1)} %copy-done.3, bf16[16,4096]{1,0:T(8,128)(2,1)} %copy-done.2, bf16[4096,896]{1,0:T(8,128)(2,1)} %wg_hbm.1, bf16[4096,896]{1,0:T(8,128)(2,1)} %wu_hbm.1, bf16[896,4096]{1,0:T(8,128)(2,1)} %wd_hbm.1), custom_call_target="tpu_custom_call" | custom-call | flops 5637144576 | bytes 22020096 | tf_op jit(solution)/shard_map/pallas_call | solution.py:455
  69.0 1.7 %broadcast_select_fusion = bf16[8,2,4096]{2,1,0:T(2,128)(2,1)} fusion(bf16[8,2,4096]{2,1,0:T(2,128)(2,1)} %shard_map.128, pred[8]{0:T(512)(128)(4,1)S(1)} %iota_compare_fusion.1), kind=kLoop, calls=%fused_computation | loop fusion | flops 65536 | bytes 262152 | tf_op jit(solution)/shard_map/jit(_where)/select_n | solution.py:518
  (4 shorter events, 0.0 us)
Async XLA Ops:
  1.0 1.6 %copy-start = (bf16[8,256,512]{2,1,0:T(8,128)(2,1)S(1)}, bf16[8,256,512]{2,1,0:T(8,128)(2,1)}, u32[]{:S(2)}) copy-start(bf16[8,256,512]{2,1,0:T(8,128)(2,1)} %k_ref.1) | copy-start | bytes 6291460
  2.6 1.6 %copy-start.1 = (bf16[8,256,512]{2,1,0:T(8,128)(2,1)S(1)}, bf16[8,256,512]{2,1,0:T(8,128)(2,1)}, u32[]{:S(2)}) copy-start(bf16[8,256,512]{2,1,0:T(8,128)(2,1)} %v_ref.1) | copy-start | bytes 6291460
  4.2 0.9 %copy-start.4 = (bf16[8,2,4096]{2,1,0:T(2,128)(2,1)S(1)}, bf16[8,2,4096]{2,1,0:T(2,128)(2,1)}, u32[]{:S(2)}) copy-start(bf16[8,2,4096]{2,1,0:T(2,128)(2,1)} %q_ref.1) | copy-start | bytes 393220
  5.1 0.9 %copy-start.5 = (bf16[8,2,4096]{2,1,0:T(2,128)(2,1)S(1)}, bf16[8,2,4096]{2,1,0:T(2,128)(2,1)}, u32[]{:S(2)}) copy-start(bf16[8,2,4096]{2,1,0:T(2,128)(2,1)} %residual_ref.1) | copy-start | bytes 393220
  6.0 0.7 %copy-start.6 = (bf16[8,2,512]{2,1,0:T(2,128)(2,1)S(1)}, bf16[8,2,512]{2,1,0:T(2,128)(2,1)}, u32[]{:S(2)}) copy-start(bf16[8,2,512]{2,1,0:T(2,128)(2,1)} %dk_ref.1) | copy-start | bytes 49156
  6.7 0.7 %copy-start.7 = (bf16[8,2,512]{2,1,0:T(2,128)(2,1)S(1)}, bf16[8,2,512]{2,1,0:T(2,128)(2,1)}, u32[]{:S(2)}) copy-start(bf16[8,2,512]{2,1,0:T(2,128)(2,1)} %dv_ref.1) | copy-start | bytes 49156
  7.4 0.7 copy-start.8
  8.1 0.7 copy-start.9
  11.4 0.6 copy-start.2
  12.0 0.7 copy-start.3

commit v3 on v2

--- a/solution.py
+++ b/solution.py
@@ -19,11 +19,11 @@
 UP, DOWN, SIDE, CORE = range(4)
 
 
-def attend_kernel(
-    C, batch, lengths_ref, q_ref, dk_ref, dv_ref, k_ref, v_ref, residual_ref, gain_ref, cos_ref, sin_ref,
-    stream_ref, normed_ref, wide_ref, heads_ref, mixed_ref,
+def attention_rows(
+    inputs, lengths_ref, cos_ref, sin_ref, batch, arrived, hidden_start,
+    stream_ref, write_normed, C, wide_ref, heads_ref, mixed_ref,
 ):
-    step = pl.program_id(0)
+    q_ref, dk_ref, dv_ref, residual_ref, gain_ref, k_ref, v_ref = inputs
     slots = k_ref.shape[1]
     requests = q_ref.shape[0]
     count = 2 * requests
@@ -38,13 +38,13 @@
     def rotate(value, cosine, sine):
         return value * cosine + pltpu.roll(value, HD // 2, 1) * sine
 
-    @pl.when(step == 0)
-    def _():
-        widen(q_ref)
-        for h in range(HEADS):
-            value = rotate(wide_ref[:, h * HD : (h + 1) * HD], cos_ref[...], sin_ref[...])
-            heads_ref[pl.ds(h, count, stride=HEADS), :] = value
-        widen(residual_ref)
+    for i in range(5):
+        arrived[i].wait()
+    widen(q_ref)
+    for h in range(HEADS):
+        value = rotate(wide_ref[:, h * HD : (h + 1) * HD], cos_ref[...], sin_ref[...])
+        heads_ref[pl.ds(h, count, stride=HEADS), :] = value
+    widen(residual_ref)
 
     late = (lax.broadcasted_iota(jnp.int32, (rows, 1), 0) // group) % 2 == 1
     column = lax.broadcasted_iota(jnp.int32, (rows, slots), 1)
@@ -58,134 +58,102 @@
             axis=0,
         )
 
-    picked = []
-    for b in range(batch):
-        r = step * batch + b
-        first_row = pl.multiple_of(r * rows, 8)
-        q = jnp.concatenate(
-            [
-                heads_ref[pl.ds(first_row + s * HEADS + g * group, group), :]
-                for g in range(KVH)
-                for s in range(2)
-            ],
-            axis=0,
-        ).astype(jnp.bfloat16)
-        scores = jnp.concatenate(
-            [
-                lax.dot_general(
-                    q[g * 2 * group : (g + 1) * 2 * group],
-                    k_ref[b, :, g * HD : (g + 1) * HD],
-                    (((1,), (1,)), ((), ())),
-                    preferred_element_type=jnp.float32,
+    for step in range(requests // batch):
+        arrived[5 + 2 * step].wait()
+        arrived[6 + 2 * step].wait()
+        if step == requests // batch - 1:
+            hidden_start()
+        picked = []
+        for b in range(batch):
+            r = step * batch + b
+            first_row = r * rows
+            q = jnp.concatenate(
+                [
+                    heads_ref[pl.ds(first_row + s * HEADS + g * group, group), :]
+                    for g in range(KVH)
+                    for s in range(2)
+                ],
+                axis=0,
+            ).astype(jnp.bfloat16)
+            scores = jnp.concatenate(
+                [
+                    lax.dot_general(
+                        q[g * 2 * group : (g + 1) * 2 * group],
+                        k_ref[r, :, g * HD : (g + 1) * HD],
+                        (((1,), (1,)), ((), ())),
+                        preferred_element_type=jnp.float32,
+                    )
+                    for g in range(KVH)
+                ],
+                axis=0,
+            ) * scale
+            scores = jnp.where(column < lengths_ref[r], scores, -jnp.inf)
+            cosine, sine = cos_ref[pl.ds(2 * r, 2), :], sin_ref[pl.ds(2 * r, 2), :]
+            fresh = dk_ref[r].astype(jnp.float32)
+            fresh = jnp.concatenate(
+                [rotate(fresh[:, g * HD : (g + 1) * HD], cosine, sine) for g in range(KVH)], axis=1
+            ).astype(jnp.bfloat16).astype(jnp.float32)
+            wide = q.astype(jnp.float32)
+            first = jnp.sum(wide * spread(fresh, 0), axis=-1, keepdims=True) * scale
+            second = jnp.sum(wide * spread(fresh, 1), axis=-1, keepdims=True) * scale
+            second = jnp.where(late, second, -jnp.inf)
+            picked.append((r, scores, first, second))
+
+        for b in range(batch):
+            r, scores, first, second = picked[b]
+            highest = jnp.maximum(jnp.max(scores, axis=-1, keepdims=True), jnp.maximum(first, second))
+            scores = jnp.exp(scores - highest)
+            first = jnp.exp(first - highest)
+            second = jnp.exp(second - highest)
+            total = 1.0 / (jnp.sum(scores, axis=-1, keepdims=True) + first + second)
+            weights = (scores * total).astype(jnp.bfloat16)
+            first = (first * total).astype(jnp.bfloat16).astype(jnp.float32)
+            second = (second * total).astype(jnp.bfloat16).astype(jnp.float32)
+            fresh = dv_ref[r].astype(jnp.float32)
+            extra = first * spread(fresh, 0) + second * spread(fresh, 1)
+            first_row = r * rows
+            for g in range(KVH):
+                at = slice(g * 2 * group, (g + 1) * 2 * group)
+                mixed = extra[at] + jnp.dot(
+                    weights[at], v_ref[r, :, g * HD : (g + 1) * HD], preferred_element_type=jnp.float32
                 )
-                for g in range(KVH)
-            ],
-            axis=0,
-        ) * scale
-        scores = jnp.where(column < lengths_ref[r], scores, -jnp.inf)
-        cosine, sine = cos_ref[pl.ds(2 * r, 2), :], sin_ref[pl.ds(2 * r, 2), :]
-        fresh = dk_ref[b].astype(jnp.float32)
-        fresh = jnp.concatenate(
-            [rotate(fresh[:, g * HD : (g + 1) * HD], cosine, sine) for g in range(KVH)], axis=1
-        ).astype(jnp.bfloat16).astype(jnp.float32)
-        wide = q.astype(jnp.float32)
-        first = jnp.sum(wide * spread(fresh, 0), axis=-1, keepdims=True) * scale
-        second = jnp.sum(wide * spread(fresh, 1), axis=-1, keepdims=True) * scale
-        second = jnp.where(late, second, -jnp.inf)
-        picked.append((r, scores, first, second))
-
-    for b in range(batch):
-        r, scores, first, second = picked[b]
-        highest = jnp.maximum(jnp.max(scores, axis=-1, keepdims=True), jnp.maximum(first, second))
-        scores = jnp.exp(scores - highest)
-        first = jnp.exp(first - highest)
-        second = jnp.exp(second - highest)
-        total = 1.0 / (jnp.sum(scores, axis=-1, keepdims=True) + first + second)
-        weights = (scores * total).astype(jnp.bfloat16)
-        first = (first * total).astype(jnp.bfloat16).astype(jnp.float32)
-        second = (second * total).astype(jnp.bfloat16).astype(jnp.float32)
-        fresh = dv_ref[b].astype(jnp.float32)
-        extra = first * spread(fresh, 0) + second * spread(fresh, 1)
-        first_row = pl.multiple_of(r * rows, 8)
-        for g in range(KVH):
-            at = slice(g * 2 * group, (g + 1) * 2 * group)
-            mixed = extra[at] + jnp.dot(
-                weights[at], v_ref[b, :, g * HD : (g + 1) * HD], preferred_element_type=jnp.float32
-            )
-            for s in range(2):
-                mixed_ref[pl.ds(first_row + s * HEADS + g * group, group), :] = mixed[
-                    s * group : (s + 1) * group
-                ]
-
-    @pl.when(step == pl.num_programs(0) - 1)
-    def _():
-        square = jnp.zeros((count, HD), jnp.float32)
-        for h in range(HEADS):
-            at = slice(h * HD, (h + 1) * HD)
-            value = wide_ref[:, at] + mixed_ref[pl.ds(h, count, stride=HEADS), :]
-            value = value.astype(jnp.bfloat16)
-            stream_ref[:, at] = value
-            value = value.astype(jnp.float32)
-            square += value * value
-        mean = jnp.sum(square, axis=-1, keepdims=True) / (HEADS * HD)
-        factor = lax.rsqrt(mean + norm_epsilon)
-        width = normed_ref.shape[2]
-        for k in range(C):
-            at = slice(k * width, (k + 1) * width)
-            normed_ref[k] = (
-                stream_ref[:, at].astype(jnp.float32) * factor * gain_ref[at].astype(jnp.float32)[None, :]
-            ).astype(jnp.bfloat16)
-
-
-def attend(C, queries, new_keys, new_values, key_cache, value_cache, residual, gain, lengths, positions):
-    requests, drafts = queries.shape[:2]
-    slots = key_cache.shape[1]
-    count = requests * drafts
-    width = HEADS * HD
-    batch = 4 if requests % 4 == 0 else 1
+                for s in range(2):
+                    mixed_ref[pl.ds(first_row + s * HEADS + g * group, group), :] = mixed[
+                        s * group : (s + 1) * group
+                    ]
+
+    square = jnp.zeros((count, HD), jnp.float32)
+    for h in range(HEADS):
+        at = slice(h * HD, (h + 1) * HD)
+        value = wide_ref[:, at] + mixed_ref[pl.ds(h, count, stride=HEADS), :]
+        value = value.astype(jnp.bfloat16)
+        stream_ref[:, at] = value
+        value = value.astype(jnp.float32)
+        square += value * value
+    mean = jnp.sum(square, axis=-1, keepdims=True) / (HEADS * HD)
+    factor = lax.rsqrt(mean + norm_epsilon)
+    width = HEADS * HD // C
+    for k in range(C):
+        at = slice(k * width, (k + 1) * width)
+        write_normed(k, (
+            stream_ref[:, at].astype(jnp.float32) * factor * gain_ref[at].astype(jnp.float32)[None, :]
+        ).astype(jnp.bfloat16))
+
+
+def turn_tables(requests, drafts, positions):
     place = jnp.arange(HD)
     frequency = rope_base ** (-2.0 * (place % (HD // 2)).astype(jnp.float32) / HD)
-    row = jnp.arange(count)
+    row = jnp.arange(requests * drafts)
     offsets = jnp.repeat(positions, drafts).astype(jnp.float32) + (row % drafts).astype(jnp.float32)
     angles = offsets[:, None] * frequency[None, :]
-    cosine = jnp.cos(angles)
-    sine = jnp.where(place[None, :] < HD // 2, -jnp.sin(angles), jnp.sin(angles))
-    whole = pl.BlockSpec(memory_space=pltpu.VMEM)
-    return pl.pallas_call(
-        functools.partial(attend_kernel, C, batch),
-        grid=(requests // batch,),
-        in_specs=[
-            pl.BlockSpec(memory_space=pltpu.SMEM),
-            whole,
-            pl.BlockSpec((batch, drafts, KVH * HD), lambda r: (r, 0, 0)),
-            pl.BlockSpec((batch, drafts, KVH * HD), lambda r: (r, 0, 0)),
-            pl.BlockSpec((batch, slots, KVH * HD), lambda r: (r, 0, 0)),
-            pl.BlockSpec((batch, slots, KVH * HD), lambda r: (r, 0, 0)),
-            whole,
-            whole,
-            whole,
-            whole,
-        ],
-        out_specs=[
-            pl.BlockSpec((count, width), lambda r: (0, 0)),
-            pl.BlockSpec((C, count, width // C), lambda r: (0, 0, 0)),
-        ],
-        out_shape=[
-            jax.ShapeDtypeStruct((count, width), jnp.bfloat16),
-            jax.ShapeDtypeStruct((C, count, width // C), jnp.bfloat16),
-        ],
-        scratch_shapes=[
-            pltpu.VMEM((count, width), jnp.float32),
-            pltpu.VMEM((count * HEADS, HD), jnp.float32),
-            pltpu.VMEM((count * HEADS, HD), jnp.float32),
-        ],
-        compiler_params=pltpu.CompilerParams(vmem_limit_bytes=32 * 1024 * 1024),
-        cost_estimate=pl.CostEstimate(flops=10**8, bytes_accessed=5 * 10**6, transcendentals=10**5),
-    )(lengths, queries, new_keys, new_values, key_cache, value_cache, residual, gain, cosine, sine)
+    sine = jnp.sin(angles)
+    return jnp.cos(angles), jnp.where(place[None, :] < HD // 2, -sine, sine)
 
 
 def feed_kernel(
-    C, Z, Y, normed_ref, stream_ref, wg_hbm, wu_hbm, wd_hbm, out_ref,
+    C, Z, Y, lengths_ref, cos_ref, sin_ref, q_hbm, dk_hbm, dv_hbm, residual_hbm, gain_hbm,
+    k_hbm, v_hbm, wg_hbm, wu_hbm, wd_hbm, out_ref,
+    q_in, dk_in, dv_in, residual_in, gain_in, k_in, v_in, stream_ref, wide, heads, mixed, in_sem,
     gath, wg, wu, wd, acc_g, acc_u, hid, part, r_core, r_side, r_line, fin,
     w_sem, ag_send, ag_recv, core_send, core_recv, side_send, side_recv, line_send, line_recv,
 ):
@@ -203,6 +171,19 @@
     targets = [up, down, side, core]
     has_up, has_down = z < Z - 1, z > 0
 
+    requests = q_in.shape[0]
+    batch = 4 if requests % 4 == 0 else 1
+    arrived = []
+    fetched = ((q_hbm, q_in), (dk_hbm, dk_in), (dv_hbm, dv_in), (residual_hbm, residual_in), (gain_hbm, gain_in))
+    for source, place in fetched:
+        arrived.append(pltpu.make_async_copy(source, place, in_sem.at[len(arrived)]))
+    for step in range(requests // batch):
+        at = pl.ds(step * batch, batch)
+        for source, place in ((k_hbm, k_in), (v_hbm, v_in)):
+            arrived.append(pltpu.make_async_copy(source.at[at], place.at[at], in_sem.at[len(arrived)]))
+    for copy in arrived:
+        copy.start()
+
     weight_copies = []
     for k in range(C):
         at = pl.ds(k * kc, kc)
@@ -211,8 +192,10 @@
     for n in range(C):
         at = pl.ds(n * width, width)
         weight_copies.append(pltpu.make_async_copy(wd_hbm.at[:, at], wd.at[:, at], w_sem.at[2, n]))
-    for copy in weight_copies:
-        copy.start()
+
+    def weights_start():
+        for copy in weight_copies:
+            copy.start()
 
     barrier = pltpu.get_barrier_semaphore()
 
@@ -232,8 +215,14 @@
         return pl.ds(pl.multiple_of(at * R, R), count * R)
 
     own = index(c, y, z)
-    for k in range(C):
-        gath[k, rows(own), :] = normed_ref[k]
+
+    def write_normed(k, value):
+        gath[k, rows(own), :] = value
+
+    attention_rows(
+        (q_in, dk_in, dv_in, residual_in, gain_in, k_in, v_in), lengths_ref, cos_ref, sin_ref,
+        batch, arrived, weights_start, stream_ref, write_normed, C, wide, heads, mixed,
+    )
 
     peers = 2 if Y == 2 else 1
     ends = jnp.logical_or(z == 0, z == Z - 1)
@@ -442,8 +431,11 @@
             pl.when(goal < z)(lambda goal=goal: line_copy(k, goal, DOWN).wait_send())
 
 
-def feed(C, Z, Y, shape, normed, stream, wg, wu, wd):
-    R, D = stream.shape
+def layer(C, Z, Y, lengths, cosine, sine, *arrays):
+    queries, new_keys, new_values, residual, gain, key_cache, value_cache, wg, wu, wd = arrays
+    shape = residual.shape
+    requests, drafts, D = shape
+    R = requests * drafts
     ff = wg.shape[1]
     N = 2 * Y * Z
     M = N * R
@@ -455,9 +447,14 @@
     return pl.pallas_call(
         functools.partial(feed_kernel, C, Z, Y),
         out_shape=jax.ShapeDtypeStruct(shape, bf16),
-        in_specs=[vmem, vmem, hbm, hbm, hbm],
+        in_specs=[pl.BlockSpec(memory_space=pltpu.SMEM), vmem, vmem] + [hbm] * 10,
         out_specs=vmem,
-        scratch_shapes=[
+        scratch_shapes=[pltpu.VMEM(array.shape, bf16) for array in arrays[:7]] + [
+            pltpu.VMEM((R, D), bf16),
+            pltpu.VMEM((R, D), jnp.float32),
+            pltpu.VMEM((R * HEADS, HD), jnp.float32),
+            pltpu.VMEM((R * HEADS, HD), jnp.float32),
+            dma((5 + 2 * requests,)),
             pltpu.VMEM((C, M, width), bf16),
             pltpu.VMEM((D, ff), bf16),
             pltpu.VMEM((D, ff), bf16),
@@ -486,7 +483,7 @@
         cost_estimate=pl.CostEstimate(
             flops=6 * M * D * ff, bytes_accessed=6 * D * ff, transcendentals=M * ff
         ),
-    )(normed, stream, wg, wu, wd)
+    )(lengths, cosine, sine, *arrays)
 
 
 def shards(
@@ -508,12 +505,11 @@
     positions,
 ):
     requests = residual_in.shape[0]
-    stream, normed = attend(
-        C, queries, new_keys, new_values, key_cache, value_cache,
-        residual_in, norm_gain,
-        cache_lengths, positions,
+    cosine, sine = turn_tables(requests, residual_in.shape[1], positions)
+    combined = layer(
+        C, Z, Y, cache_lengths, cosine, sine, queries, new_keys, new_values, residual_in, norm_gain,
+        key_cache, value_cache, gate_weight, up_weight, down_weight,
     )
-    combined = feed(C, Z, Y, residual_in.shape, normed, stream, gate_weight, up_weight, down_weight)
     live_slot = jnp.arange(requests) < live_counts[0]
     return jnp.where(live_slot[:, None, None], combined, jnp.zeros_like(combined))
 

time: 71.2 us -> 62.2 us (0.87)
  local copies, waits for them, and re-layouts: 9.21 us -> 0.15 us
    unnamed x20 -> x0, local copies, waits for them, and re-layouts: 9.05 us -> none
    pallas_call x2 -> x1, Pallas kernels: 58.3 us -> 58 us  [layer(): pl.pallas_call(functools.partial(feed_kernel, C, Z, Y), out_shape=jax.Sha...]
where the time goes in v3:
time: 62.2 us; the launch traced here: 62 us
  Pallas kernels  58 us (93%)
  other arithmetic  3.15 us (5%)
  between operations  0.67 us (1%)
    pallas_call x1, Pallas kernels, layer(): pl.pallas_call(functools.partial(feed_kernel, C, Z, Y), out_shape=jax.Sha...  58 us
    select_n x1, other arithmetic, shards(): jnp.where(live_slot[:, None, None], combined, jnp.zeros_like(combined))  1.74 us

profile of v3, /device:TPU:0, one launch (start us, length us, event | category | flops | bytes accessed | tf_op | source)
XLA Modules:
  0.0 62.0 jit_solution(14001787835652556423)
XLA Ops:
  0.0 0.7 %convert_element_type.25 = f32[8]{0:T(128)S(1)} convert(s32[8]{0:T(128)} %param.25) | non-fusion elementwise | flops 8 | bytes 64 | tf_op jit(solution)/shard_map/convert_element_type | solution.py:147
  0.7 0.1 broadcast_in_dim.27
  0.7 0.1 convert_element_type.26
  0.8 0.7 %negate_select_fusion = (f32[16,128]{1,0:T(8,128)}, f32[16,128]{1,0:T(8,128)}) fusion(f32[128]{0:T(128)S(1)} %fusion.4, f32[16]{0:T(128)S(1)} %fusion.1, pred[128]{0:T(512)(128)(4,1)S(1)} %iota_compare_fusion), kind=kLoop, calls=%fused_computation.1 | loop fusion | flops 6144 | bytes 17088 | tf_op jit(solution)/shard_map/jit(_where)/select_n | solution.py:150
  1.6 58.0 %shard_map.127 = bf16[8,2,4096]{2,1,0:T(2,128)(2,1)} custom-call(s32[8]{0:T(128)} %lengths_ref.1, f32[16,128]{1,0:T(8,128)} %get-tuple-element.6.cos_ref, f32[16,128]{1,0:T(8,128)} %get-tuple-element.5.sin_ref, bf16[8,2,4096]{2,1,0:T(2,128)(2,1)} %q_hbm.1, bf16[8,2,512]{2,1,0:T(2,128)(2,1)} %dk_hbm.1, bf16[8,2,512]{2,1,0:T(2,128)(2,1)} %dv_hbm.1, ...), custom_call_target="tpu_custom_call" | custom-call | flops 5637144576 | bytes 22020096 | tf_op jit(solution)/shard_map/pallas_call | solution.py:447
  60.2 1.7 %broadcast_select_fusion = bf16[8,2,4096]{2,1,0:T(2,128)(2,1)} fusion(bf16[8,2,4096]{2,1,0:T(2,128)(2,1)} %shard_map.127, pred[8]{0:T(512)(128)(4,1)S(1)} %iota_compare_fusion.1), kind=kLoop, calls=%fused_computation | loop fusion | flops 65536 | bytes 262152 | tf_op jit(solution)/shard_map/jit(_where)/select_n | solution.py:514
  (4 shorter events, 0.0 us)

commit v4 on v3

--- a/solution.py
+++ b/solution.py
@@ -16,7 +16,7 @@
 norm_epsilon = 1e-05
 
 MESH = pl.DeviceIdType.MESH
-UP, DOWN, SIDE, CORE = range(4)
+SIDE, CORE = range(2)
 
 
 def attention_rows(
@@ -155,7 +155,7 @@
     k_hbm, v_hbm, wg_hbm, wu_hbm, wd_hbm, out_ref,
     q_in, dk_in, dv_in, residual_in, gain_in, k_in, v_in, stream_ref, wide, heads, mixed, in_sem,
     gath, wg, wu, wd, acc_g, acc_u, hid, part, r_core, r_side, r_line, fin,
-    w_sem, ag_send, ag_recv, core_send, core_recv, side_send, side_recv, line_send, line_recv,
+    w_sem, out_send, ag_send, ag_recv, core_send, core_recv, side_send, side_recv, line_send, line_recv,
 ):
     c = lax.axis_index("attn")
     f = lax.axis_index("ffn")
@@ -164,12 +164,15 @@
     N = 2 * Y * Z
     kc = gath.shape[2]
     width = part.shape[2]
-    up = {"ffn": (z + 1) * Y + y}
-    down = {"ffn": (z - 1) * Y + y}
     side = {"ffn": z * Y + (Y - 1 - y)}
     core = {"attn": 1 - c}
-    targets = [up, down, side, core]
-    has_up, has_down = z < Z - 1, z > 0
+    targets = [side, core]
+
+    def ahead(d):
+        return lax.rem(z + d, Z)
+
+    def behind(d):
+        return lax.rem(z + Z - d, Z)
 
     requests = q_in.shape[0]
     batch = 4 if requests % 4 == 0 else 1
@@ -205,8 +208,8 @@
     greet(core)
     if Y == 2:
         greet(side)
-    pl.when(has_up)(lambda: greet(up))
-    pl.when(has_down)(lambda: greet(down))
+    for d in range(1, Z):
+        greet({"ffn": ahead(d) * Y + y})
 
     def index(cc, yy, zz):
         return (cc * Y + yy) * Z + zz
@@ -224,10 +227,14 @@
         batch, arrived, weights_start, stream_ref, write_normed, C, wide, heads, mixed,
     )
 
-    peers = 2 if Y == 2 else 1
-    ends = jnp.logical_or(z == 0, z == Z - 1)
-    pl.when(ends)(lambda: pl.semaphore_wait(barrier, peers + 1))
-    pl.when(jnp.logical_not(ends))(lambda: pl.semaphore_wait(barrier, peers + 2))
+    pl.semaphore_wait(barrier, (Z - 1) + Y)
+
+    def line_out(k, d):
+        at = gath.at[k, rows(own), :]
+        return pltpu.make_async_remote_copy(
+            src_ref=at, dst_ref=at, send_sem=out_send.at[k, d], recv_sem=ag_recv.at[k, own],
+            device_id={"ffn": ahead(d) * Y + y}, device_id_type=MESH,
+        )
 
     def ag(k, block, way):
         at = gath.at[k, rows(block), :]
@@ -237,36 +244,24 @@
         )
 
     def line_step(d, k, act):
+        block = own if d == 0 else index(c, y, behind(d))
         if d == 0:
-            pl.when(has_up)(lambda: act(k, own, UP))
-            pl.when(has_down)(lambda: act(k, own, DOWN))
-            if Y == 2:
-                act(k, own, SIDE)
-            act(k, own, CORE)
-            return
-
-        def arrived(block, way, more):
-            if act is start:
-                ag(k, block, way).wait_recv()
-            pl.when(more)(lambda: act(k, block, way))
-            if Y == 2:
-                act(k, block, SIDE)
-            act(k, block, CORE)
-
-        pl.when(z - d >= 0)(lambda: arrived(index(c, y, z - d), UP, has_up))
-        pl.when(z + d < Z)(lambda: arrived(index(c, y, z + d), DOWN, has_down))
+            for e in range(1, Z):
+                if act is start:
+                    line_out(k, e).start()
+                else:
+                    line_out(k, e).wait_send()
+        elif act is start:
+            ag(k, block, CORE).wait_recv()
+        if Y == 2:
+            act(k, block, SIDE)
+        act(k, block, CORE)
 
     def side_step(d, k, act):
-        def arrived(block):
-            if act is start:
-                ag(k, block, SIDE).wait_recv()
-            act(k, block, CORE)
-
-        if d == 0:
-            arrived(index(c, 1 - y, z))
-        else:
-            pl.when(z - d >= 0)(lambda: arrived(index(c, 1 - y, z - d)))
-            pl.when(z + d < Z)(lambda: arrived(index(c, 1 - y, z + d)))
+        block = index(c, 1 - y, behind(d))
+        if act is start:
+            ag(k, block, SIDE).wait_recv()
+        act(k, block, CORE)
 
     def start(k, block, way):
         ag(k, block, way).start()
@@ -298,18 +293,17 @@
         else:
             hid[...] = (new_g / (1.0 + jnp.exp(-new_g)) * new_u).astype(jnp.bfloat16)
 
-    lag = 2
-    for t in range(C + Z + lag):
+    for k in range(C):
+        line_step(0, k, start)
+    for k in range(C + 2):
+        for d in range(1, Z):
+            if k < C:
+                line_step(d, k, start)
         for d in range(Z):
-            if 0 <= t - d < C:
-                line_step(d, t - d, start)
-        if Y == 2:
-            for d in range(Z):
-                if 0 <= t - lag - d < C:
-                    side_step(d, t - lag - d, start)
-        k = t - lag - (Z - 1)
-        if 0 <= k < C:
-            project(k)
+            if Y == 2 and 0 <= k - 1 < C:
+                side_step(d, k - 1, start)
+        if k >= 2:
+            project(k - 2)
 
     half = Y * Z
 
@@ -327,12 +321,11 @@
             device_id=side, device_id_type=MESH,
         )
 
-    def line_copy(n, goal, way):
-        slot = goal + 1 if way == UP else goal
+    def line_copy(n, d):
         return pltpu.make_async_remote_copy(
-            src_ref=part.at[n, rows(index(c, y, goal)), :], dst_ref=r_line.at[n, rows(slot), :],
-            send_sem=line_send.at[n, goal], recv_sem=line_recv.at[n, slot],
-            device_id=targets[way], device_id_type=MESH,
+            src_ref=part.at[n, rows(index(c, y, ahead(d))), :], dst_ref=r_line.at[n, rows(d), :],
+            send_sem=line_send.at[n, d], recv_sem=line_recv.at[n, d],
+            device_id={"ffn": ahead(d) * Y + y}, device_id_type=MESH,
         )
 
     def add(n, at, other):
@@ -360,63 +353,33 @@
             side_copy(n).wait_recv()
             add(n, rows(index(c, y, 0), Z), r_side[n])
 
-    def along(n, way):
-        source = has_down if way == UP else has_up
-        for step in range(Z - 1):
-            goal = Z - 1 - step if way == UP else step
-
-            def move(goal=goal):
-                @pl.when(source)
-                def _():
-                    line_copy(n, goal, way).wait_recv()
-                    slot = goal + 1 if way == UP else goal
-                    add(n, rows(index(c, y, goal)), r_line[n, rows(slot), :])
-
-                line_copy(n, goal, way).start()
-
-            pl.when(goal > z if way == UP else goal < z)(move)
+    def along(n):
+        for d in range(1, Z):
+            line_copy(n, d).start()
 
     def complete(n):
         at = pl.ds(n * width, width)
         fin[...] = part[n, rows(own), :].astype(jnp.float32)
 
-        @pl.when(has_down)
-        def _():
-            line_copy(n, z, UP).wait_recv()
-            fin[...] += r_line[n, rows(z + 1), :].astype(jnp.float32)
-
-        @pl.when(has_up)
-        def _():
-            line_copy(n, z, DOWN).wait_recv()
-            fin[...] += r_line[n, rows(z), :].astype(jnp.float32)
+        for d in range(1, Z):
+            line_copy(n, d).wait_recv()
+            fin[...] += r_line[n, rows(d), :].astype(jnp.float32)
 
         fin[...] += stream_ref[:, at].astype(jnp.float32)
         drafts = out_ref.shape[1]
         for r in range(out_ref.shape[0]):
             out_ref[r, :, at] = fin[r * drafts : (r + 1) * drafts, :].astype(jnp.bfloat16)
 
-    if C == 1:
-        produce(0)
-        after_core(0)
-        after_side(0)
-        along(0, UP)
-        along(0, DOWN)
-        complete(0)
-    else:
-        for t in range(C + Z + 4):
-            if t < C:
-                produce(t)
-            if 0 <= t - 1 < C:
-                after_core(t - 1)
-            if 0 <= t - 2 < C:
-                after_side(t - 2)
-            for hop in range(Z - 1):
-                n = t - 2 - hop
-                if 0 <= n < C:
-                    pl.when(z == hop)(functools.partial(along, n, UP))
-                    pl.when(z == Z - 1 - hop)(functools.partial(along, n, DOWN))
-            if 0 <= t - 2 - Z < C:
-                complete(t - 2 - Z)
+    for t in range(C + 4):
+        if t < C:
+            produce(t)
+        if 0 <= t - 1 < C:
+            after_core(t - 1)
+        if 0 <= t - 2 < C:
+            after_side(t - 2)
+            along(t - 2)
+        if 0 <= t - 4 < C:
+            complete(t - 4)
 
     for k in range(C):
         for d in range(Z):
@@ -426,9 +389,8 @@
         core_copy(k).wait_send()
         if Y == 2:
             side_copy(k).wait_send()
-        for goal in range(Z):
-            pl.when(goal > z)(lambda goal=goal: line_copy(k, goal, UP).wait_send())
-            pl.when(goal < z)(lambda goal=goal: line_copy(k, goal, DOWN).wait_send())
+        for d in range(1, Z):
+            line_copy(k, d).wait_send()
 
 
 def layer(C, Z, Y, lengths, cosine, sine, *arrays):
@@ -468,7 +430,8 @@
             pltpu.VMEM((C, (Z + 1) * R, width), bf16),
             pltpu.VMEM((R, width), jnp.float32),
             dma((3, C)),
-            dma((4, C, N)),
+            dma((C, Z)),
+            dma((2, C, N)),
             dma((C, N)),
             dma((C,)),
             dma((C,)),

time: 62.2 us -> 55.8 us (0.90)
  Pallas kernels: 58 us -> 51.6 us
    pallas_call x1, Pallas kernels: 58 us -> 51.6 us  [layer(): pl.pallas_call(functools.partial(feed_kernel, C, Z, Y), out_shape=jax.Sha...]
where the time goes in v4:
time: 55.8 us; the launch traced here: 55.6 us
  Pallas kernels  51.6 us (92%)
  other arithmetic  3.15 us (6%)
  between operations  0.67 us (1%)
    pallas_call x1, Pallas kernels, layer(): pl.pallas_call(functools.partial(feed_kernel, C, Z, Y), out_shape=jax.Sha...  51.6 us
    select_n x1, other arithmetic, shards(): jnp.where(live_slot[:, None, None], combined, jnp.zeros_like(combined))  1.74 us

profile of v4, /device:TPU:0, one launch (start us, length us, event | category | flops | bytes accessed | tf_op | source)
XLA Modules:
  0.0 55.6 jit_solution(5577301348427803557)
XLA Ops:
  0.0 0.7 %convert_element_type.25 = f32[8]{0:T(128)S(1)} convert(s32[8]{0:T(128)} %param.25) | non-fusion elementwise | flops 8 | bytes 64 | tf_op jit(solution)/shard_map/convert_element_type | solution.py:147
  0.7 0.1 broadcast_in_dim.27
  0.7 0.1 convert_element_type.26
  0.8 0.7 %negate_select_fusion = (f32[16,128]{1,0:T(8,128)}, f32[16,128]{1,0:T(8,128)}) fusion(f32[128]{0:T(128)S(1)} %fusion.4, f32[16]{0:T(128)S(1)} %fusion.1, pred[128]{0:T(512)(128)(4,1)S(1)} %iota_compare_fusion), kind=kLoop, calls=%fused_computation.1 | loop fusion | flops 6144 | bytes 17088 | tf_op jit(solution)/shard_map/jit(_where)/select_n | solution.py:150
  1.6 51.6 %shard_map.127 = bf16[8,2,4096]{2,1,0:T(2,128)(2,1)} custom-call(s32[8]{0:T(128)} %lengths_ref.1, f32[16,128]{1,0:T(8,128)} %get-tuple-element.6.cos_ref, f32[16,128]{1,0:T(8,128)} %get-tuple-element.5.sin_ref, bf16[8,2,4096]{2,1,0:T(2,128)(2,1)} %q_hbm.1, bf16[8,2,512]{2,1,0:T(2,128)(2,1)} %dk_hbm.1, bf16[8,2,512]{2,1,0:T(2,128)(2,1)} %dv_hbm.1, ...), custom_call_target="tpu_custom_call" | custom-call | flops 5637144576 | bytes 22020096 | tf_op jit(solution)/shard_map/pallas_call | solution.py:409
  53.9 1.7 %broadcast_select_fusion = bf16[8,2,4096]{2,1,0:T(2,128)(2,1)} fusion(bf16[8,2,4096]{2,1,0:T(2,128)(2,1)} %shard_map.127, pred[8]{0:T(512)(128)(4,1)S(1)} %iota_compare_fusion.1), kind=kLoop, calls=%fused_computation | loop fusion | flops 65536 | bytes 262152 | tf_op jit(solution)/shard_map/jit(_where)/select_n | solution.py:477
  (4 shorter events, 0.0 us)

commit v5 on v4

--- a/solution.py
+++ b/solution.py
@@ -151,7 +151,7 @@
 
 
 def feed_kernel(
-    C, Z, Y, lengths_ref, cos_ref, sin_ref, q_hbm, dk_hbm, dv_hbm, residual_hbm, gain_hbm,
+    C, Z, Y, live_ref, lengths_ref, cos_ref, sin_ref, q_hbm, dk_hbm, dv_hbm, residual_hbm, gain_hbm,
     k_hbm, v_hbm, wg_hbm, wu_hbm, wd_hbm, out_ref,
     q_in, dk_in, dv_in, residual_in, gain_in, k_in, v_in, stream_ref, wide, heads, mixed, in_sem,
     gath, wg, wu, wd, acc_g, acc_u, hid, part, r_core, r_side, r_line, fin,
@@ -365,8 +365,9 @@
             line_copy(n, d).wait_recv()
             fin[...] += r_line[n, rows(d), :].astype(jnp.float32)
 
-        fin[...] += stream_ref[:, at].astype(jnp.float32)
         drafts = out_ref.shape[1]
+        live = lax.broadcasted_iota(jnp.int32, fin.shape, 0) < live_ref[0] * drafts
+        fin[...] = jnp.where(live, fin[...] + stream_ref[:, at].astype(jnp.float32), 0.0)
         for r in range(out_ref.shape[0]):
             out_ref[r, :, at] = fin[r * drafts : (r + 1) * drafts, :].astype(jnp.bfloat16)
 
@@ -393,7 +394,7 @@
             line_copy(k, d).wait_send()
 
 
-def layer(C, Z, Y, lengths, cosine, sine, *arrays):
+def layer(C, Z, Y, live, lengths, cosine, sine, *arrays):
     queries, new_keys, new_values, residual, gain, key_cache, value_cache, wg, wu, wd = arrays
     shape = residual.shape
     requests, drafts, D = shape
@@ -409,7 +410,7 @@
     return pl.pallas_call(
         functools.partial(feed_kernel, C, Z, Y),
         out_shape=jax.ShapeDtypeStruct(shape, bf16),
-        in_specs=[pl.BlockSpec(memory_space=pltpu.SMEM), vmem, vmem] + [hbm] * 10,
+        in_specs=[pl.BlockSpec(memory_space=pltpu.SMEM)] * 2 + [vmem, vmem] + [hbm] * 10,
         out_specs=vmem,
         scratch_shapes=[pltpu.VMEM(array.shape, bf16) for array in arrays[:7]] + [
             pltpu.VMEM((R, D), bf16),
@@ -446,7 +447,7 @@
         cost_estimate=pl.CostEstimate(
             flops=6 * M * D * ff, bytes_accessed=6 * D * ff, transcendentals=M * ff
         ),
-    )(lengths, cosine, sine, *arrays)
+    )(live, lengths, cosine, sine, *arrays)
 
 
 def shards(
@@ -469,12 +470,10 @@
 ):
     requests = residual_in.shape[0]
     cosine, sine = turn_tables(requests, residual_in.shape[1], positions)
-    combined = layer(
-        C, Z, Y, cache_lengths, cosine, sine, queries, new_keys, new_values, residual_in, norm_gain,
+    return layer(
+        C, Z, Y, live_counts, cache_lengths, cosine, sine, queries, new_keys, new_values, residual_in, norm_gain,
         key_cache, value_cache, gate_weight, up_weight, down_weight,
     )
-    live_slot = jnp.arange(requests) < live_counts[0]
-    return jnp.where(live_slot[:, None, None], combined, jnp.zeros_like(combined))
 
 
 def solution(mesh):

time: 55.8 us -> 55.8 us (level)
  other arithmetic: 3.15 us -> 1.41 us
  local copies, waits for them, and re-layouts: 0.15 us -> 1.8 us
    select_n x1 -> x0, other arithmetic: 1.74 us -> none  [shards(): jnp.where(live_slot[:, None, None], combined, jnp.zeros_like(combined))]
    unnamed x0 -> x1, local copies, waits for them, and re-layouts: none -> 1.65 us
where the time goes in v5:
time: 55.8 us; the launch traced here: 55.5 us
  Pallas kernels  51.6 us (92%)
  local copies, waits for them, and re-layouts  1.8 us (3%)
  other arithmetic  1.41 us (3%)
  between operations  0.66 us (1%)
    pallas_call x1, Pallas kernels, layer(): pl.pallas_call(functools.partial(feed_kernel, C, Z, Y), out_shape=jax.Sha...  51.6 us
    unnamed x1, local copies, waits for them, and re-layouts  1.65 us

profile of v5, /device:TPU:0, one launch (start us, length us, event | category | flops | bytes accessed | tf_op | source)
XLA Modules:
  0.0 55.5 jit_solution(15449644648277076171)
XLA Ops:
  0.7 0.7 %convert_element_type.25 = f32[8]{0:T(128)S(1)} convert(s32[8]{0:T(128)} %param.25) | non-fusion elementwise | flops 8 | bytes 64 | tf_op jit(solution)/shard_map/convert_element_type | solution.py:147
  1.3 0.1 broadcast_in_dim.14
  1.4 0.1 convert_element_type.26
  1.5 0.7 %negate_select_fusion = (f32[16,128]{1,0:T(8,128)}, f32[16,128]{1,0:T(8,128)}) fusion(f32[128]{0:T(128)S(1)} %fusion.4, f32[16]{0:T(128)S(1)} %fusion.1, pred[128]{0:T(512)(128)(4,1)S(1)} %iota_compare_fusion), kind=kLoop, calls=%fused_computation | loop fusion | flops 6144 | bytes 17088 | tf_op jit(solution)/shard_map/jit(_where)/select_n | solution.py:150
  2.2 51.6 %shard_map.127 = bf16[8,2,4096]{2,1,0:T(2,128)(2,1)} custom-call(s32[1]{0:T(128)S(6)} %copy.15.live_ref, s32[8]{0:T(128)} %lengths_ref.1, f32[16,128]{1,0:T(8,128)} %get-tuple-element.6.cos_ref, f32[16,128]{1,0:T(8,128)} %get-tuple-element.5.sin_ref, bf16[8,2,4096]{2,1,0:T(2,128)(2,1)} %q_hbm.1, bf16[8,2,512]{2,1,0:T(2,128)(2,1)} %dk_hbm.1, ...), custom_call_target="tpu_custom_call" | custom-call | flops 5637144576 | bytes 22020096 | tf_op jit(solution)/shard_map/pallas_call | solution.py:410
  53.9 1.7 %copy.16 = bf16[8,2,4096]{2,1,0:T(2,128)(2,1)} copy(bf16[8,2,4096]{2,1,0:T(2,128)(2,1)} %shard_map.127) | data formatting | bytes 262144
  (3 shorter events, 0.0 us)
